TPU v7x, 512 devices: a whole 4x8x8 slice. The times are simulated.
512 devices in a mesh: tile: 64 (over x, z, core), tm: 8 (over y).
Axes of the slice: x: 4, y: 8, z: 8, core: 2. Of those that a mesh axis runs over, the one named last changes fastest.
Arguments:
- model: bfloat16 [2, 16384, 1024], P(None, ('tile', 'tm')), may hold values from -6 to 6
- kern_rows: bfloat16 [24576, 32, 256], P(('tile', 'tm')), may hold values from -1 to 1
- kern_cols: bfloat16 [24576, 128, 256], P(('tile', 'tm')), may hold values from -0.5 to 0.5
- visibilities: bfloat16 [24576, 2, 256], P(('tile', 'tm')), may hold values from -6 to 6
- owner_tile: int32 [24576, 1], P(('tile', 'tm')), may hold values from 0 to 63; in each aligned block of 48 rows (0 to 47, 48 to 95, ...) at most 2 rows name the same one
- row_offset: int32 [24576], P(('tile', 'tm')), may hold values from 0 to 224
- col_offset: int32 [24576], P(('tile', 'tm')), may hold values from 0 to 896
Outputs:
- dirty_grid: float32 [2, 16384, 1024], P(None, ('tile', 'tm'))
- residual_vis: float32 [24576, 2, 256], P(('tile', 'tm'))
Inputs may be any that keep to these rules, and one draw needn't show every extreme that they name: `owner_tile`: among the 48 blocks of one device no tile is named more than 2 times, and some device names a tile exactly 2 times.
All inputs are finite; a program needn't handle non-finite values.
Results may differ from a plain program's by a relative error of at most 0.0026.
Values may be sent and summed in bfloat16 or wider, within the bound.
A program may use at most 128 MiB of HBM per device.

v0:
```python
import jax
import jax.numpy as jnp
from jax import lax
from jax.sharding import PartitionSpec as P


def degrid_regrid(patches, kern_rows, kern_wide, visibilities):
    sampled = jnp.einsum("scuv,svj->scuj", patches, kern_wide, preferred_element_type=jnp.float32)
    row_weights = kern_rows.astype(jnp.float32)[:, None]
    predicted = jnp.sum(row_weights * sampled, axis=2)
    residual = visibilities.astype(jnp.float32) - predicted
    weighted = (row_weights * residual[:, :, None, :]).astype(jnp.bfloat16)
    subgrid = jnp.einsum("scuj,svj->scuv", weighted, kern_wide, preferred_element_type=jnp.float32)
    return (residual, subgrid)


def widen(kern_cols, col_at):
    sub_cols = kern_cols.shape[1]
    remain = col_at % sub_cols
    wide_index = jnp.arange(2 * sub_cols, dtype=jnp.int32)
    narrow_index = jnp.arange(sub_cols, dtype=jnp.int32)
    placing = (
        wide_index[None, :, None] == remain[:, None, None] + narrow_index[None, None, :]
    ).astype(jnp.bfloat16)
    kern_wide = jnp.einsum("bwv,bvj->bwj", placing, kern_cols, preferred_element_type=jnp.float32)
    return (kern_wide.astype(jnp.bfloat16), col_at - remain)


def extract(padded_panel, row_at, col_base, sub_rows, sub_cols):
    anchor = jnp.zeros((), jnp.int32)

    def single(row_one, col_one):
        return lax.dynamic_slice(
            padded_panel, (anchor, row_one, col_one), (2, sub_rows, 2 * sub_cols)
        )

    return jax.vmap(single)(row_at, col_base)


def add_patches(total, subgrids, row_at, col_base):
    sub_rows = subgrids.shape[2]
    wide_cols = subgrids.shape[3]
    anchor = jnp.zeros((), jnp.int32)

    def add_one(index, running):
        corner = (anchor, row_at[index], col_base[index])
        window = lax.dynamic_slice(running, corner, (2, sub_rows, wide_cols))
        return lax.dynamic_update_slice(running, window + subgrids[index], corner)

    return lax.fori_loop(0, subgrids.shape[0], add_one, total)


def shards(model, kern_rows, kern_cols, visibilities, owner_tile, row_offset, col_offset):
    tile_count = lax.axis_size("tile")
    blocks_here = owner_tile.shape[0]
    capacity = (blocks_here + tile_count - 1) // tile_count + 1
    sub_rows = kern_rows.shape[1]
    sub_cols = kern_cols.shape[1]
    owners = owner_tile[:, 0]
    onehot = (owners[:, None] == jnp.arange(tile_count, dtype=jnp.int32)[None, :]).astype(jnp.int32)
    earlier = jnp.cumsum(onehot, axis=0) - onehot
    slot_index = jnp.sum(earlier * onehot, axis=1)

    def to_slots(values):
        buffer = jnp.zeros((tile_count, capacity) + values.shape[1:], values.dtype)
        return buffer.at[owners, slot_index].set(values)

    def flatten(values):
        return values.reshape((tile_count * capacity,) + values.shape[2:])

    tile_panel = lax.all_gather(model, "tm", axis=1, tiled=True)
    padded_panel = jnp.pad(tile_panel, ((0, 0), (0, 0), (0, sub_cols)))
    arrived = (
        lax.all_to_all(to_slots(kern_rows), "tile", split_axis=0, concat_axis=0, tiled=True),
        lax.all_to_all(to_slots(kern_cols), "tile", split_axis=0, concat_axis=0, tiled=True),
        lax.all_to_all(to_slots(visibilities), "tile", split_axis=0, concat_axis=0, tiled=True),
        lax.all_to_all(to_slots(row_offset), "tile", split_axis=0, concat_axis=0, tiled=True),
        lax.all_to_all(to_slots(col_offset), "tile", split_axis=0, concat_axis=0, tiled=True),
    )
    rows_got, cols_got, vis_got, row_at, col_at = [flatten(item) for item in arrived]
    kern_wide, col_base = widen(cols_got, col_at)
    patches = extract(padded_panel, row_at, col_base, sub_rows, sub_cols)
    residual, subgrid = degrid_regrid(patches, rows_got, kern_wide, vis_got)
    shaped = residual.reshape((tile_count, capacity) + residual.shape[1:])
    returned = lax.all_to_all(shaped, "tile", split_axis=0, concat_axis=0, tiled=True)
    residual_vis = returned[owners, slot_index]
    dirty_wide = add_patches(jnp.zeros(padded_panel.shape, jnp.float32), subgrid, row_at, col_base)
    dirty_tile = dirty_wide[:, :, : tile_panel.shape[2]]
    dirty_part = lax.psum_scatter(dirty_tile, "tm", scatter_dimension=1, tiled=True)
    return (dirty_part, residual_vis)


def solution(mesh):
    placed = (
        P(None, ("tile", "tm"), None),
        P(("tile", "tm"), None, None),
        P(("tile", "tm"), None, None),
        P(("tile", "tm"), None, None),
        P(("tile", "tm"), None),
        P(("tile", "tm")),
        P(("tile", "tm")),
    )
    return jax.shard_map(
        shards,
        mesh=mesh,
        in_specs=placed,
        out_specs=(P(None, ("tile", "tm"), None), P(("tile", "tm"), None, None)),
        check_vma=False,
    )
```

profile of v0, /device:TPU:6, one launch (start us, length us, event | category | flops | bytes accessed | tf_op | source)
XLA Modules:
  0.0 1479.4 jit_solution(7903601086806402700)
XLA Ops:
  9.6 4.4 scatter_fusion
  14.7 14.0 all-to-all-start
  28.8 4.4 scatter_fusion.1
  33.9 2.3 all-to-all-done
  36.3 8.0 all-to-all-start.1
  45.9 6.8 scatter_fusion.2
  52.7 10.3 all-to-all-start.2
  63.8 4.3 broadcast_in_dim.14
  68.1 9.7 scatter_fusion.4
  78.5 6.5 scatter_fusion.3
  87.6 20.2 %all-gather.2.cloned.1.call-done = bf16[2,256,1024]{2,1,0:T(8,128)(2,1)} async-done(((bf16[2,32,1024]{2,1,0:T(8,128)(2,1)}), bf16[2,256,1024]{2,1,0:T(8,128)(2,1)}) %all-gather.2.cloned.1.call-update) | async-done | bytes 1048592 | tf_op jit(solution)/shard_map/all_gather | solution.py:71
  109.1 2.9 all-to-all-done.2
  112.0 8.5 all-to-all-start.4
  120.5 340.8 %while.15 = (s32[]{:T(128)}, bf16[2,256,1152]{2,1,0:T(8,128)(2,1)S(1)}, s32[128,3]{0,1:T(4,128)S(1)}, bf16[128,2,32,256]{3,2,1,0:T(8,128)(2,1)}, s32[]{:T(128)}) while((s32[]{:T(128)}, bf16[2,256,1152]{2,1,0:T(8,128)(2,1)S(1)}, s32[128,3]{0,1:T(4,128)S(1)}, bf16[128,2,32,256]{3,2,1,0:T(8,128)(2,1)}, s32[]{:T(128)}) %tuple.49), condition=%wide.while_cond, body=%wide.while_body.sunk | while | flops 2 | bytes 67177 | solution.py:33
  123.8 2.0 bitcast_dynamic-update-slice_fusion.2
  129.2 2.0 bitcast_dynamic-update-slice_fusion.2
  139.8 2.0 bitcast_dynamic-update-slice_fusion.2
  145.1 2.0 bitcast_dynamic-update-slice_fusion.2
  150.4 2.0 bitcast_dynamic-update-slice_fusion.2
  171.7 2.0 bitcast_dynamic-update-slice_fusion.2
  177.1 2.0 bitcast_dynamic-update-slice_fusion.2
  182.4 2.0 bitcast_dynamic-update-slice_fusion.2
  187.7 2.0 bitcast_dynamic-update-slice_fusion.2
  193.0 2.0 bitcast_dynamic-update-slice_fusion.2
  198.4 2.0 bitcast_dynamic-update-slice_fusion.2
  209.0 2.0 bitcast_dynamic-update-slice_fusion.2
  214.3 2.0 bitcast_dynamic-update-slice_fusion.2
  225.0 2.0 bitcast_dynamic-update-slice_fusion.2
  230.3 2.0 bitcast_dynamic-update-slice_fusion.2
  238.3 2.0 bitcast_dynamic-update-slice_fusion.2
  241.0 2.0 bitcast_dynamic-update-slice_fusion.2
  251.6 2.0 bitcast_dynamic-update-slice_fusion.2
  256.9 2.0 bitcast_dynamic-update-slice_fusion.2
  262.3 2.0 bitcast_dynamic-update-slice_fusion.2
  272.9 2.0 bitcast_dynamic-update-slice_fusion.2
  275.6 2.0 bitcast_dynamic-update-slice_fusion.2
  283.6 2.0 bitcast_dynamic-update-slice_fusion.2
  299.5 2.0 bitcast_dynamic-update-slice_fusion.2
  304.8 2.0 bitcast_dynamic-update-slice_fusion.2
  315.5 2.0 bitcast_dynamic-update-slice_fusion.2
  320.8 2.0 bitcast_dynamic-update-slice_fusion.2
  326.1 2.0 bitcast_dynamic-update-slice_fusion.2
  342.1 2.0 bitcast_dynamic-update-slice_fusion.2
  347.4 2.0 bitcast_dynamic-update-slice_fusion.2
  350.1 2.0 bitcast_dynamic-update-slice_fusion.2
  352.8 2.0 bitcast_dynamic-update-slice_fusion.2
  363.4 2.0 bitcast_dynamic-update-slice_fusion.2
  379.4 2.0 bitcast_dynamic-update-slice_fusion.2
  384.7 2.0 bitcast_dynamic-update-slice_fusion.2
  395.4 2.0 bitcast_dynamic-update-slice_fusion.2
  411.3 2.0 bitcast_dynamic-update-slice_fusion.2
  427.3 2.0 bitcast_dynamic-update-slice_fusion.2
  440.6 2.0 bitcast_dynamic-update-slice_fusion.2
  443.3 2.0 bitcast_dynamic-update-slice_fusion.2
  456.6 2.0 bitcast_dynamic-update-slice_fusion.2
  459.3 2.0 bitcast_dynamic-update-slice_fusion.2
  461.3 2.6 bitcast_convert_fusion
  463.8 10.3 all-to-all-start.3
  474.4 11.4 fusion.5
  485.8 10.9 multiply_reduce_fusion
  496.9 11.6 fusion
  508.7 917.3 %while.14 = (s32[]{:T(128)}, f32[2,256,1152]{2,1,0:T(8,128)S(1)}, s32[128]{0:T(128)S(1)}, s32[128]{0:T(128)S(1)}, f32[128,2,32,256]{3,2,1,0:T(8,128)}, /*index=5*/s32[]{:T(128)}, s32[]{:T(128)}, s32[]{:T(128)}, s32[]{:T(128)}) while((s32[]{:T(128)}, f32[2,256,1152]{2,1,0:T(8,128)S(1)}, s32[128]{0:T(128)S(1)}, s32[128]{0:T(128)S(1)}, ...), condition=%wide.region_9.10_spmd, body=%wide.region_8.9_spmd.sunk | while | flops 16392 | bytes 327881 | solution.py:50
  1427.9 21.2 %all_to_all.38 = f32[64,2,2,256]{3,2,1,0:T(2,128)S(1)} all-to-all(f32[64,2,2,256]{3,2,1,0:T(2,128)S(1)} %convert_subtract_fusion), channel_id=1, replica_groups=mesh['tile'=64,'tm'=8] {'tile'}, dimensions={0} | all-to-all | bytes 524288 | tf_op jit(solution)/shard_map/all_to_all | solution.py:85
  1450.7 21.9 %reduce-scatter.2.cloned.1.call-done = f32[2,32,1024]{2,1,0:T(8,128)} async-done(((f32[2,256,1024]{2,1,0:T(8,128)}), f32[2,32,1024]{2,1,0:T(8,128)}) %reduce-scatter.2.cloned.1.call-update) | async-done | bytes 262160 | tf_op jit(solution)/shard_map/reduce_scatter | solution.py:89
  (894 shorter events, 687.5 us)
Async XLA Ops:
  7.2 38.8 %copy-start = (bf16[48,32,256]{2,1,0:T(8,128)(2,1)S(1)}, bf16[48,32,256]{2,1,0:T(8,128)(2,1)}, u32[]{:S(2)}) copy-start(bf16[48,32,256]{2,1,0:T(8,128)(2,1)} %param.10) | copy-start | bytes 2359300
  14.7 21.5 %all-to-all-start = ((s32[64,1,2]{2,1,0:T(1,128)}), s32[64,1,2]{2,1,0:T(1,128)S(1)}, u32[]{:S(2)}, u32[]{:S(2)}) async-start(s32[64,1,2]{2,1,0:T(1,128)} %copy.17), calls=%async_computation | async-start | bytes 65536 | tf_op jit(solution)/shard_map/all_to_all | solution.py:77
  36.3 16.5 %all-to-all-start.1 = ((s32[64,1,2]{2,1,0:T(1,128)}), s32[64,1,2]{2,1,0:T(1,128)S(1)}, u32[]{:S(2)}, u32[]{:S(2)}) async-start(s32[64,1,2]{2,1,0:T(1,128)} %copy.18), calls=%async_computation.1 | async-start | bytes 65536 | tf_op jit(solution)/shard_map/all_to_all | solution.py:78
  52.7 59.3 %all-to-all-start.2 = ((bf16[64,2,32,256]{3,2,1,0:T(8,128)(2,1)}), bf16[64,2,32,256]{3,2,1,0:T(8,128)(2,1)S(1)}, u32[]{:S(2)}, u32[]{:S(2)}) async-start(bf16[64,2,32,256]{3,2,1,0:T(8,128)(2,1)} %scatter_fusion.2), calls=%async_computation.2 | async-start | bytes 4194304 | tf_op jit(solution)/shard_map/all_to_all | solution.py:74
  63.1 44.7 %all-gather.2.cloned.1.call-start = ((), (), s32[]{:S(2)}) async-start(), calls=%async_computation.7 | async-start | bytes 1179648 | tf_op jit(solution)/shard_map/all_gather | solution.py:71
  68.1 10.4 copy-start.1
  112.0 351.8 %all-to-all-start.4 = ((bf16[64,2,128,256]{3,2,1,0:T(8,128)(2,1)}), bf16[64,2,128,256]{3,2,1,0:T(8,128)(2,1)}, u32[]{:S(2)}, u32[]{:S(2)}) async-start(bf16[64,2,128,256]{3,2,1,0:T(8,128)(2,1)} %scatter_fusion.4), calls=%async_computation.4 | async-start | bytes 16777216 | tf_op jit(solution)/shard_map/all_to_all | solution.py:75
  463.8 32.9 %all-to-all-start.3 = ((bf16[64,2,2,256]{3,2,1,0:T(2,128)(2,1)}), bf16[64,2,2,256]{3,2,1,0:T(2,128)(2,1)S(1)}, u32[]{:S(2)}, u32[]{:S(2)}) async-start(bf16[64,2,2,256]{3,2,1,0:T(2,128)(2,1)} %scatter_fusion.3), calls=%async_computation.3 | async-start | bytes 262144 | tf_op jit(solution)/shard_map/all_to_all | solution.py:76
  474.2 998.4 %reduce-scatter.2.cloned.1.call-start = ((), (), s32[]{:S(2)}) async-start(), calls=%async_computation.8 | async-start | bytes 2359296 | tf_op jit(solution)/shard_map/reduce_scatter | solution.py:89
Sparse Core Ops, SparseCore 0:
  66.0 41.7 all-gather.1
  1427.8 44.6 reduce-scatter.1
where the time goes:
time: 1500 us; the launch traced here: 1480 us
  local copies, waits for them, and re-layouts  683 us (46%)
  loops' own time  502 us (33%)
  other arithmetic  126 us (8%)
  starting transfers between devices  51.4 us (3%)
  waiting for transfers between devices  48 us (3%)
  matrix products  34 us (2%)
  blocking collectives  21.2 us (1%)
    another operation x1, loops' own time, add_patches(): return lax.fori_loop(0, subgrids.shape[0], add_one, total)  501 us
    gather x384, local copies, waits for them, and re-layouts  341 us
    dynamic_slice x256, local copies, waits for them, and re-layouts, add_one(): corner = (anchor, row_at[index], col_base[index])  151 us
    dynamic_update_slice x128, local copies, waits for them, and re-layouts, add_one(): return lax.dynamic_update_slice(running, window + subgrids[index], corner)  146 us
    add x128, other arithmetic, add_one(): return lax.dynamic_update_slice(running, window + subgrids[index], corner)  120 us
    scatter x5, local copies, waits for them, and re-layouts, to_slots(): return buffer.at[owners, slot_index].set(values)  31.9 us
  transfers between devices with their start and end apart: 7, of which 4 were waited for; matrix products, arithmetic and copies ran while one was open for 27% of the time, Pallas kernels for 0%

commit v1 on v0

v1 whole, which is shorter than its diff:
```python
import functools

import jax
import jax.numpy as jnp
from jax import lax
from jax.experimental import pallas as pl
from jax.experimental.pallas import tpu as pltpu
from jax.sharding import PartitionSpec as P

VMEM_LIMIT = 48 * 1024 * 1024


def corner(row, col, shape, sub_rows, sub_cols):
    top = jnp.minimum(row // 8, (shape[0] - sub_rows) // 8 - 1) * 8
    base = jnp.minimum(col // sub_cols, shape[1] // sub_cols - 2) * sub_cols
    return pl.multiple_of(top, 8), row - top, pl.multiple_of(base, sub_cols), col - base


def extract_kernel(req_ref, panel_ref, *rest, slots, shards):
    outs, wide = rest[:slots], rest[slots]
    sub_rows, sub_cols = outs[0].shape[2], outs[0].shape[3]
    shard_rows = panel_ref.shape[2]
    tiles = outs[0].shape[0]
    for m in range(shards):
        wide[:, m * shard_rows : (m + 1) * shard_rows, :] = panel_ref[m].astype(jnp.float32)
    for s in range(slots):

        @pl.loop(0, tiles, unroll=2)
        def _(o):
            row = jnp.maximum(req_ref[(o * slots + s) * 2], 0)
            col = jnp.maximum(req_ref[(o * slots + s) * 2 + 1], 0)
            top, down, base, right = corner(row, col, wide.shape[1:], sub_rows, sub_cols)
            for c in range(2):
                window = wide[c, pl.ds(top, sub_rows + 8), pl.ds(base, 2 * sub_cols)]
                window = pltpu.roll(window, lax.rem(sub_rows + 8 - down, sub_rows + 8), 0)[:sub_rows]
                window = pltpu.roll(window, lax.rem(2 * sub_cols - right, 2 * sub_cols), 1)
                outs[s][o, c] = window[:, :sub_cols].astype(jnp.bfloat16)


def block_kernel(order_ref, count_ref, patch_ref, rows_ref, cols_ref, vis_ref, *rest, step):
    sub_ref, res_ref = rest[-2:]
    sub_rows, sub_cols = patch_ref.shape[2], patch_ref.shape[3]
    vis_n = rows_ref.shape[2]
    if len(rest) == 3:
        res_ref[...] = rest[0][...]

    @pl.loop(0, count_ref[0])
    def _(i):
        for k in range(step):
            b = order_ref[2 * (i * step + k)]
            o = order_ref[2 * (i * step + k) + 1]
            patch = patch_ref[o].reshape(2 * sub_rows, sub_cols)
            cols = cols_ref[b]
            sampled = jnp.dot(patch, cols, preferred_element_type=jnp.float32)
            weights = rows_ref[b].astype(jnp.float32)
            sampled = sampled.reshape(2, sub_rows, vis_n)
            predicted = jnp.sum(weights[None] * sampled, axis=1)
            residual = vis_ref[b].astype(jnp.float32) - predicted
            res_ref[b] = residual
            weighted = (weights[None] * residual[:, None, :]).astype(jnp.bfloat16)
            weighted = weighted.reshape(2 * sub_rows, vis_n)
            sub = lax.dot_general(
                weighted, cols, (((1,), (1,)), ((), ())), preferred_element_type=jnp.float32
            )
            sub_ref[o] = sub.astype(jnp.bfloat16).reshape(2, sub_rows, sub_cols)


def add_kernel(req_ref, *rest, slots):
    subs, acc = rest[:slots], rest[slots]
    sub_rows, sub_cols = subs[0].shape[2], subs[0].shape[3]
    tiles = subs[0].shape[0]
    acc[...] = jnp.zeros_like(acc)
    for s in range(slots):

        @pl.loop(0, tiles)
        def _(o):
            row = req_ref[(o * slots + s) * 2]
            col = req_ref[(o * slots + s) * 2 + 1]

            @pl.when(row >= 0)
            def _():
                top, down, base, right = corner(row, col, acc.shape[1:], sub_rows, sub_cols)
                for c in range(2):
                    sub = subs[s][o, c].astype(jnp.float32)
                    window = jnp.concatenate([sub, jnp.zeros_like(sub)], axis=1)
                    window = pltpu.roll(window, right, 1)
                    window = jnp.concatenate([window, jnp.zeros((8, 2 * sub_cols), jnp.float32)], axis=0)
                    window = pltpu.roll(window, down, 0)
                    at = (c, pl.ds(top, sub_rows + 8), pl.ds(base, 2 * sub_cols))
                    acc[at] = acc[at] + window


def smem():
    return pl.BlockSpec(memory_space=pltpu.SMEM)


def vmem():
    return pl.BlockSpec(memory_space=pltpu.VMEM)


def shards(model, kern_rows, kern_cols, visibilities, owner_tile, row_offset, col_offset):
    tiles = lax.axis_size("tile")
    blocks = owner_tile.shape[0]
    slots = (blocks + tiles - 1) // tiles + 1
    sub_rows = kern_rows.shape[1]
    sub_cols = kern_cols.shape[1]
    grid_cols = model.shape[2]
    params = pltpu.CompilerParams(vmem_limit_bytes=VMEM_LIMIT)
    step = 4

    owners = owner_tile[:, 0]
    ids = jnp.arange(blocks, dtype=jnp.int32)
    earlier = (owners[:, None] == owners[None, :]) & (ids[None, :] < ids[:, None])
    slot_of = jnp.sum(earlier.astype(jnp.int32), axis=1)
    hot = (
        (owners[None, None, :] == jnp.arange(tiles, dtype=jnp.int32)[:, None, None])
        & (slot_of[None, None, :] == jnp.arange(slots, dtype=jnp.int32)[None, :, None])
    ).astype(jnp.int32)
    request = (
        jnp.stack(
            [
                jnp.sum(hot * (row_offset + 1)[None, None, :], axis=2),
                jnp.sum(hot * (col_offset + 1)[None, None, :], axis=2),
            ],
            axis=-1,
        )
        - 1
    )
    got = lax.all_to_all(request, "tile", split_axis=0, concat_axis=0, tiled=True).reshape(-1)
    panel = lax.all_gather(model, "tm", axis=0)
    group = panel.shape[0]

    patches = pl.pallas_call(
        functools.partial(extract_kernel, slots=slots, shards=group),
        out_shape=[jax.ShapeDtypeStruct((tiles, 2, sub_rows, sub_cols), jnp.bfloat16)] * slots,
        in_specs=[smem(), vmem()],
        out_specs=[vmem()] * slots,
        scratch_shapes=[pltpu.VMEM((2, group * model.shape[1], grid_cols), jnp.float32)],
        compiler_params=params,
        name="extract",
    )(got, panel)

    residual = None
    returned = []
    for s in range(slots):
        arrived = lax.all_to_all(patches[s], "tile", split_axis=0, concat_axis=0, tiled=True)
        mine = slot_of == s
        place = jnp.cumsum(mine.astype(jnp.int32)) - 1
        count = jnp.sum(mine.astype(jnp.int32))
        spots = jnp.arange(-(-blocks // step) * step, dtype=jnp.int32)
        wanted = jnp.minimum(spots, jnp.maximum(count - 1, 0))
        pick = (mine[None, :] & (place[None, :] == wanted[:, None])).astype(jnp.int32)
        order = jnp.stack([jnp.sum(pick * ids[None, :], axis=1), jnp.sum(pick * owners[None, :], axis=1)], axis=-1)
        turns = (count + step - 1) // step
        args = [order.reshape(-1), turns.reshape(1), arrived, kern_rows, kern_cols, visibilities]
        specs = [smem(), smem()] + [vmem()] * 4
        aliases = {}
        if residual is not None:
            args.append(residual)
            specs.append(vmem())
            aliases = {len(args) - 1: 1}
        sub, residual = pl.pallas_call(
            functools.partial(block_kernel, step=step),
            out_shape=[
                jax.ShapeDtypeStruct((tiles, 2, sub_rows, sub_cols), jnp.bfloat16),
                jax.ShapeDtypeStruct((blocks, 2, kern_rows.shape[2]), jnp.float32),
            ],
            in_specs=specs,
            out_specs=[vmem(), vmem()],
            input_output_aliases=aliases,
            compiler_params=params,
            name="blocks",
        )(*args)
        returned.append(lax.all_to_all(sub, "tile", split_axis=0, concat_axis=0, tiled=True))

    dirty = pl.pallas_call(
        functools.partial(add_kernel, slots=slots),
        out_shape=jax.ShapeDtypeStruct((2, group * model.shape[1], grid_cols), jnp.float32),
        in_specs=[smem()] + [vmem()] * slots,
        out_specs=vmem(),
        compiler_params=params,
        name="add",
    )(got, *returned)
    dirty_part = lax.psum_scatter(dirty, "tm", scatter_dimension=1, tiled=True)
    return (dirty_part, residual)


def solution(mesh):
    placed = (
        P(None, ("tile", "tm"), None),
        P(("tile", "tm"), None, None),
        P(("tile", "tm"), None, None),
        P(("tile", "tm"), None, None),
        P(("tile", "tm"), None),
        P(("tile", "tm")),
        P(("tile", "tm")),
    )
    return jax.shard_map(
        shards,
        mesh=mesh,
        in_specs=placed,
        out_specs=(P(None, ("tile", "tm"), None), P(("tile", "tm"), None, None)),
        check_vma=False,
    )
```

time: 1500 us -> 272 us (0.18); the launches traced: 1480 us -> 271 us
  local copies, waits for them, and re-layouts: 683 us -> 8.07 us
  loops' own time: 502 us -> 0 us
  other arithmetic: 126 us -> 3.73 us
  blocking collectives: 21.2 us -> 94 us
  waiting for transfers between devices: 48 us -> 106 us
  starting transfers between devices: 51.4 us -> 16.7 us
  matrix products: 34 us -> 0 us
  Pallas kernels: 0 us -> 26.1 us
    another operation x2 -> x0, loops' own time: 502 us -> none  [the longest x1 501 us: add_patches(): return lax.fori_loop(0, subgrids.shape[0], add_one, total)]
    gather x385 -> x0, local copies, waits for them, and re-layouts: 342 us -> none
    dynamic_slice x256 -> x0, local copies, waits for them, and re-layouts: 151 us -> none  [add_one(): corner = (anchor, row_at[index], col_base[index])]
    dynamic_update_slice x128 -> x0, local copies, waits for them, and re-layouts: 146 us -> none  [add_one(): return lax.dynamic_update_slice(running, window + subgrids[index], corner)]
    add x129 -> x1, other arithmetic: 120 us -> 0.68 us  [shards(): col_offset + 1]
    all_to_all x1 -> x3, blocking collectives: 21.2 us -> 94 us  [the longest x1 37.7 us: shards(): lax.all_to_all(patches[s], 'tile', split_axis=0, concat_axis=0, tiled=True)]
    all_to_all x5 -> x2, starting transfers between devices: 51.1 us -> 16.6 us  [the longest x1 8.29 us: shards(): lax.all_to_all(patches[s], 'tile', split_axis=0, concat_axis=0, tiled=True)]
    dot_general x3 -> x0, matrix products: 34 us -> none  [the longest x1 11.6 us: degrid_regrid(): jnp.einsum('scuj,svj->scuv', weighted, kern_wide, preferred_element_type=...]
  transfers between devices with their start and end apart: 7 -> 4, of which waited for: 4 -> 4; matrix products, arithmetic and copies ran while one was open for 27% -> 2% of each run, Pallas kernels for 0% -> 4%
where the time goes in v1:
time: 272 us; the launch traced here: 271 us
  waiting for transfers between devices  106 us (39%)
  blocking collectives  94 us (35%)
  Pallas kernels  26.1 us (10%)
  between operations  16.8 us (6%)
  starting transfers between devices  16.7 us (6%)
  local copies, waits for them, and re-layouts  8.07 us (3%)
  other arithmetic  3.73 us (1%)
    reduce_scatter x1, waiting for transfers between devices, shards(): dirty_part = lax.psum_scatter(dirty, 'tm', scatter_dimension=1, tiled=True)  48.5 us
    all_to_all x1, blocking collectives, shards(): lax.all_to_all(patches[s], 'tile', split_axis=0, concat_axis=0, tiled=True)  37.7 us
    all_to_all x1, blocking collectives, shards(): lax.all_to_all(sub, 'tile', split_axis=0, concat_axis=0, tiled=True)  34.7 us
    all_gather x1, waiting for transfers between devices, shards(): panel = lax.all_gather(model, 'tm', axis=0)  22.7 us
    all_to_all x1, blocking collectives, shards(): lax.all_to_all(request, 'tile', split_axis=0, concat_axis=0, tiled=True)  21.6 us
    all_to_all x1, waiting for transfers between devices, shards(): lax.all_to_all(sub, 'tile', split_axis=0, concat_axis=0, tiled=True)  20.6 us
    all_to_all x1, waiting for transfers between devices, shards(): lax.all_to_all(patches[s], 'tile', split_axis=0, concat_axis=0, tiled=True)  13 us
    pallas_call x2, Pallas kernels, shards(): pl.pallas_call(functools.partial(block_kernel, step=step), out_shape=[jax...  9.49 us
  transfers between devices with their start and end apart: 4, of which 4 were waited for; matrix products, arithmetic and copies ran while one was open for 2% of the time, Pallas kernels for 4%

profile of v1, /device:TPU:6, one launch (start us, length us, event | category | flops | bytes accessed | tf_op | source)
XLA Modules:
  0.0 271.0 jit_solution(18150813828744858511)
XLA Ops:
  7.2 0.0 copy-start
  7.2 0.0 all-gather.3.cloned.1.call-start
  7.2 0.7 all-gather.3.cloned.1.call-update
  7.9 1.0 convert_reduce_fusion
  9.0 0.7 broadcast_add_fusion
  9.7 0.7 iota_compare_fusion.1
  10.4 0.1 fusion
  10.5 0.1 copy.25
  10.6 21.6 %all_to_all.25 = s32[64,2,2]{1,2,0:T(2,128)S(1)} all-to-all(s32[64,2,2]{1,2,0:T(2,128)S(1)} %copy.25), channel_id=1, replica_groups=mesh['tile'=64,'tm'=8] {'tile'}, dimensions={0} | all-to-all | bytes 2048 | tf_op jit(solution)/shard_map/all_to_all | solution.py:129
  32.2 0.5 copy.26
  32.7 0.1 reshape.159.req_ref
  32.9 22.7 %all-gather.3.cloned.1.call-done = bf16[16,32,1024]{2,1,0:T(8,128)(2,1)} async-done(((bf16[2,32,1024]{2,1,0:T(8,128)(2,1)}), bf16[16,32,1024]{2,1,0:T(8,128)(2,1)}) %all-gather.3.cloned.1.call-update) | async-done | bytes 1048592 | tf_op jit(solution)/shard_map/all_gather | solution.py:130
  55.6 0.0 copy-start.4
  55.6 1.2 copy-done.4
  56.8 0.0 copy-start.9
  56.8 0.0 copy-start.8
  56.8 8.6 %extract.1 = (bf16[64,2,32,128]{3,2,1,0:T(8,128)(2,1)S(1)}, bf16[64,2,32,128]{3,2,1,0:T(8,128)(2,1)S(1)}) custom-call(s32[256]{0:T(256)S(1)} %reshape.159.req_ref, bf16[8,2,32,1024]{3,2,1,0:T(8,128)(2,1)S(1)} %bitcast.14), custom_call_target="tpu_custom_call" | custom-call | tf_op jit(solution)/shard_map/extract/pallas_call | solution.py:133
  65.4 0.0 copy-start.5
  65.4 37.7 %all_to_all.26.patch_ref = bf16[64,2,32,128]{3,2,1,0:T(8,128)(2,1)} all-to-all(bf16[64,2,32,128]{3,2,1,0:T(8,128)(2,1)S(1)} %get-tuple-element.8), channel_id=1, replica_groups=mesh['tile'=64,'tm'=8] {'tile'}, dimensions={0} | all-to-all | bytes 2097152 | tf_op jit(solution)/shard_map/all_to_all | solution.py:146
  103.1 0.0 copy-done.5
  103.1 8.3 %all-to-all-start.3 = ((bf16[64,2,32,128]{3,2,1,0:T(8,128)(2,1)}), bf16[64,2,32,128]{3,2,1,0:T(8,128)(2,1)}, u32[]{:S(2)}, u32[]{:S(2)}) async-start(bf16[64,2,32,128]{3,2,1,0:T(8,128)(2,1)} %copy-done.5), calls=%async_computation.3 | async-start | bytes 2097152 | tf_op jit(solution)/shard_map/all_to_all | solution.py:146
  111.4 0.6 convert_reduce_fusion.1
  114.0 0.1 copy.27
  114.1 0.1 reduce-window.16
  114.2 0.1 copy.29
  114.3 0.1 reduce-window.17
  114.4 0.1 add_reduce_fusion
  114.5 0.0 copy-done.9
  114.5 0.2 select_reduce_fusion.1
  114.7 0.1 copy.28
  114.8 0.1 reshape.160.order_ref
  114.9 0.0 copy-done
  115.0 0.0 copy-done.8
  115.0 0.0 copy-start.1
  115.0 1.2 copy-done.1
  116.2 0.0 copy-start.2
  116.2 1.1 copy-done.2
  117.3 6.6 %blocks.2 = (bf16[64,2,32,128]{3,2,1,0:T(8,128)(2,1)S(1)}, f32[48,2,256]{2,1,0:T(2,128)}) custom-call(s32[96]{0:T(128)S(1)} %reshape.160.order_ref, s32[1]{0:T(128)} %bitcast.6.count_ref, bf16[64,2,32,128]{3,2,1,0:T(8,128)(2,1)S(1)} %copy-done.1, bf16[48,32,256]{2,1,0:T(8,128)(2,1)S(1)} %copy-done.2, bf16[48,128,256]{2,1,0:T(8,128)(2,1)S(1)} %copy-done, ...), custom_call_target="tpu_custom_call" | custom-call | tf_op jit(solution)/shard_map/blocks/pallas_call | solution.py:162
  123.9 0.0 copy-start.6
  123.9 1.0 copy-done.6
  124.9 13.0 %all-to-all-done.3.patch_ref = bf16[64,2,32,128]{3,2,1,0:T(8,128)(2,1)} async-done(((bf16[64,2,32,128]{3,2,1,0:T(8,128)(2,1)}), bf16[64,2,32,128]{3,2,1,0:T(8,128)(2,1)}, u32[]{:S(2)}, u32[]{:S(2)}) %all-to-all-start.3) | async-done | bytes 1048608 | tf_op jit(solution)/shard_map/all_to_all | solution.py:146
  138.0 8.3 %all-to-all-start.2 = ((bf16[64,2,32,128]{3,2,1,0:T(8,128)(2,1)}), bf16[64,2,32,128]{3,2,1,0:T(8,128)(2,1)}, u32[]{:S(2)}, u32[]{:S(2)}) async-start(bf16[64,2,32,128]{3,2,1,0:T(8,128)(2,1)} %copy-done.6), calls=%async_computation.2 | async-start | bytes 2097152 | tf_op jit(solution)/shard_map/all_to_all | solution.py:174
  146.3 0.0 reduce-scatter.2.cloned.1.call-start
  147.0 0.1 copy.30
  147.1 0.1 reshape.162.order_ref
  147.2 0.0 copy-start.3
  147.2 1.1 copy-done.3
  148.4 2.9 %blocks.3 = (bf16[64,2,32,128]{3,2,1,0:T(8,128)(2,1)S(1)}, f32[48,2,256]{2,1,0:T(2,128)}) custom-call(s32[96]{0:T(128)S(1)} %reshape.162.order_ref, s32[1]{0:T(128)} %bitcast.11.count_ref, bf16[64,2,32,128]{3,2,1,0:T(8,128)(2,1)} %all-to-all-done.3.patch_ref, bf16[48,32,256]{2,1,0:T(8,128)(2,1)S(1)} %copy-done.3, ...), custom_call_target="tpu_custom_call", output_to_operand_aliasing={{1}: (6, {})} | custom-call | tf_op jit(solution)/shard_map/blocks/pallas_call | solution.py:162
  151.2 0.0 copy-start.7
  151.2 1.0 copy-done.7
  152.2 20.6 %all-to-all-done.2.rest_0_ = bf16[64,2,32,128]{3,2,1,0:T(8,128)(2,1)} async-done(((bf16[64,2,32,128]{3,2,1,0:T(8,128)(2,1)}), bf16[64,2,32,128]{3,2,1,0:T(8,128)(2,1)}, u32[]{:S(2)}, u32[]{:S(2)}) %all-to-all-start.2) | async-done | bytes 1048608 | tf_op jit(solution)/shard_map/all_to_all | solution.py:174
  172.8 34.7 %all_to_all.27.rest_1_ = bf16[64,2,32,128]{3,2,1,0:T(8,128)(2,1)S(1)} all-to-all(bf16[64,2,32,128]{3,2,1,0:T(8,128)(2,1)} %copy-done.7), channel_id=1, replica_groups=mesh['tile'=64,'tm'=8] {'tile'}, dimensions={0} | all-to-all | bytes 2097152 | tf_op jit(solution)/shard_map/all_to_all | solution.py:174
  207.6 8.0 %add.47 = f32[2,256,1024]{2,1,0:T(8,128)} custom-call(s32[256]{0:T(256)S(1)} %reshape.159.req_ref, bf16[64,2,32,128]{3,2,1,0:T(8,128)(2,1)} %all-to-all-done.2.rest_0_, bf16[64,2,32,128]{3,2,1,0:T(8,128)(2,1)S(1)} %all_to_all.27.rest_1_), custom_call_target="tpu_custom_call" | custom-call | tf_op jit(solution)/shard_map/add/pallas_call | solution.py:176
  215.6 0.0 reduce-scatter.2.cloned.1.call-update
  215.6 48.5 %reduce-scatter.2.cloned.1.call-done = f32[2,32,1024]{2,1,0:T(8,128)} async-done(((f32[2,256,1024]{2,1,0:T(8,128)}), f32[2,32,1024]{2,1,0:T(8,128)}) %reduce-scatter.2.cloned.1.call-update) | async-done | bytes 262160 | tf_op jit(solution)/shard_map/reduce_scatter | solution.py:184
  (6 shorter events, 0.0 us)
Async XLA Ops:
  7.2 107.8 %copy-start = (bf16[48,128,256]{2,1,0:T(8,128)(2,1)S(1)}, bf16[48,128,256]{2,1,0:T(8,128)(2,1)}, u32[]{:S(2)}) copy-start(bf16[48,128,256]{2,1,0:T(8,128)(2,1)} %cols_ref.3) | copy-start | bytes 9437188
  7.2 48.4 %all-gather.3.cloned.1.call-start = ((), (), s32[]{:S(2)}) async-start(), calls=%async_computation.7 | async-start | bytes 1179648 | tf_op jit(solution)/shard_map/all_gather | solution.py:130
  55.6 1.2 copy-start.4
  56.8 57.6 %copy-start.9 = (s32[48,1]{0,1:T(1,128)S(1)}, s32[48,1]{0,1:T(1,128)}, u32[]{:S(2)}) copy-start(s32[48,1]{0,1:T(1,128)} %param.11) | copy-start | bytes 580
  56.8 58.1 %copy-start.8 = (bf16[48,2,256]{2,1,0:T(2,128)(2,1)S(1)}, bf16[48,2,256]{2,1,0:T(2,128)(2,1)}, u32[]{:S(2)}) copy-start(bf16[48,2,256]{2,1,0:T(2,128)(2,1)} %vis_ref.3) | copy-start | bytes 147460
  65.4 37.7 %copy-start.5 = (bf16[64,2,32,128]{3,2,1,0:T(8,128)(2,1)}, bf16[64,2,32,128]{3,2,1,0:T(8,128)(2,1)S(1)}, u32[]{:S(2)}) copy-start(bf16[64,2,32,128]{3,2,1,0:T(8,128)(2,1)S(1)} %get-tuple-element.10) | copy-start | bytes 3145732
  103.1 34.9 %all-to-all-start.3 = ((bf16[64,2,32,128]{3,2,1,0:T(8,128)(2,1)}), bf16[64,2,32,128]{3,2,1,0:T(8,128)(2,1)}, u32[]{:S(2)}, u32[]{:S(2)}) async-start(bf16[64,2,32,128]{3,2,1,0:T(8,128)(2,1)} %copy-done.5), calls=%async_computation.3 | async-start | bytes 2097152 | tf_op jit(solution)/shard_map/all_to_all | solution.py:146
  115.0 1.2 copy-start.1
  116.2 1.1 copy-start.2
  123.9 1.0 copy-start.6
  138.0 34.9 %all-to-all-start.2 = ((bf16[64,2,32,128]{3,2,1,0:T(8,128)(2,1)}), bf16[64,2,32,128]{3,2,1,0:T(8,128)(2,1)}, u32[]{:S(2)}, u32[]{:S(2)}) async-start(bf16[64,2,32,128]{3,2,1,0:T(8,128)(2,1)} %copy-done.6), calls=%async_computation.2 | async-start | bytes 2097152 | tf_op jit(solution)/shard_map/all_to_all | solution.py:174
  146.3 117.9 %reduce-scatter.2.cloned.1.call-start = ((), (), s32[]{:S(2)}) async-start(), calls=%async_computation.6 | async-start | bytes 2359296 | tf_op jit(solution)/shard_map/reduce_scatter | solution.py:184
  147.2 1.1 copy-start.3
  151.2 1.0 copy-start.7
Sparse Core Ops, SparseCore 0:
  10.1 45.4 all-gather.2
  215.7 48.3 reduce-scatter.1

commit v2 on v0

v2 whole, which is shorter than its diff:
```python
import functools

import jax
import jax.numpy as jnp
from jax import lax
from jax.experimental import pallas as pl
from jax.experimental.pallas import tpu as pltpu
from jax.sharding import PartitionSpec as P

VMEM_LIMIT = 48 * 1024 * 1024
MESH = pl.DeviceIdType.MESH


def corner(row, col, shape, sub_rows, sub_cols):
    top = jnp.minimum(row // 8, (shape[0] - sub_rows) // 8 - 1) * 8
    base = jnp.minimum(col // sub_cols, shape[1] // sub_cols - 2) * sub_cols
    return pl.multiple_of(top, 8), row - top, pl.multiple_of(base, sub_cols), col - base


def major_kernel(
    tiles, group, slots,
    inv_ref, pos_ref, req_ref, model_ref, rows_hbm, cols_hbm, vis_hbm,
    back_ref, res_ref, asked,
    panel, cells, asked_s, patch_out, patch_in, sub_out, rows_ref, cols_ref, vis_ref, res_slots,
    kern_sem, smem_sem, ask_send, ask_recv, ring_send, ring_recv, patch_send, patch_recv, back_send, back_recv,
):
    me = lax.axis_index("tile")
    tm = lax.axis_index("tm")
    sub_rows, sub_cols = patch_in.shape[3], patch_in.shape[4]
    shard_rows = model_ref.shape[1]
    vis_n = rows_ref.shape[2]
    right, left = lax.rem(tm + 1, group), lax.rem(tm + group - 1, group)
    width = 3 if (tiles - 1) % 3 == 0 else 1

    loads = [
        pltpu.make_async_copy(src, dst, kern_sem.at[i])
        for i, (src, dst) in enumerate(((rows_hbm, rows_ref), (cols_hbm, cols_ref), (vis_hbm, vis_ref)))
    ]
    for load in loads:
        load.start()

    barrier = pltpu.get_barrier_semaphore()

    @pl.loop(1, tiles)
    def _(k):
        pl.semaphore_signal(barrier, inc=1, device_id=(lax.rem(me + k, tiles), tm), device_id_type=MESH)

    near = [right, left] if group > 2 else [right]
    for other in near:
        pl.semaphore_signal(barrier, inc=1, device_id=(me, other), device_id_type=MESH)
    pl.semaphore_wait(barrier, tiles - 1 + len(near))

    def to_tile(src, dst, send, recv, peer, mine):
        return pltpu.make_async_remote_copy(
            src_ref=src.at[peer], dst_ref=dst.at[mine], send_sem=send.at[peer], recv_sem=recv.at[mine],
            device_id=(peer, tm), device_id_type=MESH,
        )

    def ring(way, step, c):
        shard = lax.rem(tm - step + group, group) if way == 0 else lax.rem(tm + step, group)
        src = model_ref.at[c] if step == 0 else panel.at[shard, c]
        return pltpu.make_async_remote_copy(
            src_ref=src, dst_ref=panel.at[shard, c],
            send_sem=ring_send.at[way, step, c], recv_sem=ring_recv.at[way, step, c],
            device_id=(me, right if way == 0 else left), device_id_type=MESH,
        )

    hops = (group // 2, (group - 1) // 2)

    def arrived(way, step, c):
        shard = lax.rem(tm - step - 1 + group, group) if way == 0 else lax.rem(tm + step + 1, group)
        return pltpu.make_async_remote_copy(
            src_ref=panel.at[shard, c], dst_ref=panel.at[shard, c],
            send_sem=ring_send.at[way, step, c], recv_sem=ring_recv.at[way, step, c],
            device_id=(me, right if way == 0 else left), device_id_type=MESH,
        ), shard

    for c in range(2):
        for way in range(2):
            if hops[way] > 0:
                ring(way, 0, c).start()

    @pl.loop(1, tiles)
    def _(k):
        to_tile(req_ref, asked, ask_send, ask_recv, lax.rem(me + k, tiles), me).start()

    asked[me] = req_ref[me]

    def spread(c, shard, values):
        for h in range(shard_rows // 16):
            for t in range(values.shape[1] // sub_cols):
                cells[c, shard * (shard_rows // 16) + h, t] = values[
                    h * 16 : (h + 1) * 16, t * sub_cols : (t + 1) * sub_cols
                ]

    for c in range(2):
        spread(c, tm, model_ref[c])
    for step in range(hops[0]):
        for c in range(2):
            for way in range(2):
                if step < hops[way]:
                    copy, shard = arrived(way, step, c)
                    copy.wait_recv()
                    if step + 1 < hops[way]:
                        ring(way, step + 1, c).start()
                    spread(c, shard, panel[shard, c])

    @pl.loop(1, tiles)
    def _(k):
        peer = lax.rem(me + k, tiles)
        to_tile(asked, asked, ask_send, ask_recv, peer, peer).wait_recv()

    to_smem = pltpu.make_async_copy(asked, asked_s, smem_sem)
    to_smem.start()
    to_smem.wait()

    tall, broad = sub_rows + 16, 2 * sub_cols
    row_gap = lax.broadcasted_iota(jnp.int32, (sub_rows, tall), 1) - lax.broadcasted_iota(
        jnp.int32, (sub_rows, tall), 0
    )
    col_gap = lax.broadcasted_iota(jnp.int32, (broad, sub_cols), 0) - lax.broadcasted_iota(
        jnp.int32, (broad, sub_cols), 1
    )

    def cut(peer, target):
        for s in range(slots):
            row = jnp.maximum(asked_s[peer, 0, 2 * s], 0)
            col = jnp.maximum(asked_s[peer, 0, 2 * s + 1], 0)
            top = jnp.minimum(lax.div(row, 16), cells.shape[1] - tall // 16)
            base = jnp.minimum(lax.div(col, sub_cols), cells.shape[2] - 2)
            window = jnp.concatenate(
                [
                    jnp.concatenate([cells[c, top + i, base + j] for c in range(2) for j in range(2)], axis=1)
                    for i in range(tall // 16)
                ],
                axis=0,
            )
            pick_rows = (row_gap == row - 16 * top).astype(jnp.float32).astype(jnp.bfloat16)
            pick_cols = (col_gap == col - sub_cols * base).astype(jnp.float32).astype(jnp.bfloat16)
            window = jnp.dot(pick_rows, window, preferred_element_type=jnp.float32).astype(jnp.bfloat16)
            window = jnp.concatenate([window[:, :broad], window[:, broad:]], axis=0)
            window = jnp.dot(window, pick_cols, preferred_element_type=jnp.float32).astype(jnp.bfloat16)
            target[peer, s] = window.reshape(2, sub_rows, sub_cols)

    @pl.loop(0, (tiles - 1) // width)
    def _(i):
        peers = [lax.rem(me + 1 + i * width + w, tiles) for w in range(width)]
        for peer in peers:
            cut(peer, patch_out)
        for peer in peers:
            to_tile(patch_out, patch_in, patch_send, patch_recv, peer, me).start()

    cut(me, patch_in)
    for load in loads:
        load.wait()

    def work(peer, target):
        for s in range(slots):
            b = inv_ref[peer * slots + s]
            patch = patch_in[peer, s].reshape(2 * sub_rows, sub_cols)
            cols = cols_ref[b]
            sampled = jnp.dot(patch, cols, preferred_element_type=jnp.float32)
            weights = rows_ref[b].astype(jnp.float32)
            sampled = sampled.reshape(2, sub_rows, vis_n)
            predicted = jnp.sum(weights[None] * sampled, axis=1)
            residual = vis_ref[b].astype(jnp.float32) - predicted
            res_slots[peer * slots + s] = residual
            weighted = (weights[None] * residual[:, None, :]).astype(jnp.bfloat16)
            weighted = weighted.reshape(2 * sub_rows, vis_n)
            sub = lax.dot_general(
                weighted, cols, (((1,), (1,)), ((), ())), preferred_element_type=jnp.float32
            )
            target[peer, s] = sub.astype(jnp.bfloat16).reshape(2, sub_rows, sub_cols)

    work(me, back_ref)

    @pl.loop(0, (tiles - 1) // width)
    def _(i):
        peers = [lax.rem(me + tiles - 1 - i * width - w, tiles) for w in range(width)]
        for peer in peers:
            to_tile(patch_out, patch_in, patch_send, patch_recv, peer, peer).wait_recv()
        for peer in peers:
            work(peer, sub_out)
        for peer in peers:
            to_tile(sub_out, back_ref, back_send, back_recv, peer, me).start()

    @pl.loop(0, res_ref.shape[0], unroll=4)
    def _(b):
        res_ref[b] = res_slots[pos_ref[b]]

    for c in range(2):
        for way in range(2):
            for step in range(hops[way]):
                ring(way, step, c).wait_send()

    @pl.loop(1, tiles)
    def _(k):
        peer = lax.rem(me + k, tiles)
        to_tile(req_ref, asked, ask_send, ask_recv, peer, me).wait_send()
        to_tile(patch_out, patch_in, patch_send, patch_recv, peer, me).wait_send()
        to_tile(sub_out, back_ref, back_send, back_recv, peer, me).wait_send()
        to_tile(sub_out, back_ref, back_send, back_recv, peer, peer).wait_recv()


def add_kernel(req_ref, subs, acc, *, slots):
    tiles, sub_rows, sub_cols = subs.shape[0], subs.shape[3], subs.shape[4]
    acc[...] = jnp.zeros_like(acc)

    @pl.loop(0, tiles * slots)
    def _(i):
        row = req_ref[2 * i]
        col = req_ref[2 * i + 1]

        @pl.when(row >= 0)
        def _():
            top, down, base, right = corner(row, col, acc.shape[1:], sub_rows, sub_cols)
            for c in range(2):
                sub = subs[i // slots, lax.rem(i, slots), c].astype(jnp.float32)
                window = jnp.concatenate([sub, jnp.zeros_like(sub)], axis=1)
                window = pltpu.roll(window, right, 1)
                window = jnp.concatenate([window, jnp.zeros((8, 2 * sub_cols), jnp.float32)], axis=0)
                window = pltpu.roll(window, down, 0)
                at = (c, pl.ds(top, sub_rows + 8), pl.ds(base, 2 * sub_cols))
                acc[at] = acc[at] + window


def smem():
    return pl.BlockSpec(memory_space=pltpu.SMEM)


def vmem():
    return pl.BlockSpec(memory_space=pltpu.VMEM)


def anywhere():
    return pl.BlockSpec(memory_space=pl.ANY)


def shards(model, kern_rows, kern_cols, visibilities, owner_tile, row_offset, col_offset):
    tiles = lax.axis_size("tile")
    group = lax.axis_size("tm")
    blocks = owner_tile.shape[0]
    slots = (blocks + tiles - 1) // tiles + 1
    sub_rows = kern_rows.shape[1]
    sub_cols = kern_cols.shape[1]
    vis_n = kern_rows.shape[2]
    shard_rows, grid_cols = model.shape[1:]
    tile_rows = group * shard_rows

    owners = owner_tile[:, 0]
    ids = jnp.arange(blocks, dtype=jnp.int32)
    earlier = (owners[:, None] == owners[None, :]) & (ids[None, :] < ids[:, None])
    place = owners * slots + jnp.sum(earlier.astype(jnp.int32), axis=1)
    hot = (place[None, :] == jnp.arange(tiles * slots, dtype=jnp.int32)[:, None]).astype(jnp.int32)
    inverse = jnp.sum(hot * ids[None, :], axis=1)
    wanted = jnp.stack([row_offset, col_offset], axis=0)
    request = (jnp.sum(hot[:, None, :] * (wanted + 1)[None], axis=2) - 1).reshape(tiles, 1, slots * 2)
    request = jnp.pad(request, ((0, 0), (0, 0), (0, 128 - slots * 2)))

    pair = (tiles, slots, 2, sub_rows, sub_cols)
    hops = max(group // 2, 1)
    dma = pltpu.SemaphoreType.DMA
    returned, residual, asked = pl.pallas_call(
        functools.partial(major_kernel, tiles, group, slots),
        out_shape=[
            jax.ShapeDtypeStruct(pair, jnp.bfloat16),
            jax.ShapeDtypeStruct((blocks, 2, vis_n), jnp.float32),
            jax.ShapeDtypeStruct((tiles, 1, 128), jnp.int32),
        ],
        in_specs=[smem(), smem(), vmem(), vmem(), anywhere(), anywhere(), anywhere()],
        out_specs=[vmem(), vmem(), vmem()],
        scratch_shapes=[
            pltpu.VMEM((group, 2, shard_rows, grid_cols), jnp.bfloat16),
            pltpu.VMEM((2, tile_rows // 16, grid_cols // sub_cols, 16, sub_cols), jnp.bfloat16),
            pltpu.SMEM((tiles, 1, 128), jnp.int32),
            pltpu.VMEM(pair, jnp.bfloat16),
            pltpu.VMEM(pair, jnp.bfloat16),
            pltpu.VMEM(pair, jnp.bfloat16),
            pltpu.VMEM(kern_rows.shape, jnp.bfloat16),
            pltpu.VMEM(kern_cols.shape, jnp.bfloat16),
            pltpu.VMEM(visibilities.shape, jnp.bfloat16),
            pltpu.VMEM((tiles * slots, 2, vis_n), jnp.float32),
            dma((3,)),
            dma,
            dma((tiles,)),
            dma((tiles,)),
            dma((2, hops, 2)),
            dma((2, hops, 2)),
            dma((tiles,)),
            dma((tiles,)),
            dma((tiles,)),
            dma((tiles,)),
        ],
        compiler_params=pltpu.CompilerParams(
            collective_id=0, has_side_effects=True, vmem_limit_bytes=VMEM_LIMIT
        ),
        name="major",
    )(inverse, place, request, model, kern_rows, kern_cols, visibilities)

    dirty = pl.pallas_call(
        functools.partial(add_kernel, slots=slots),
        out_shape=jax.ShapeDtypeStruct((2, tile_rows, grid_cols), jnp.float32),
        in_specs=[smem(), vmem()],
        out_specs=vmem(),
        compiler_params=pltpu.CompilerParams(vmem_limit_bytes=VMEM_LIMIT),
        name="add",
    )(asked[:, 0, : slots * 2].reshape(-1), returned)
    dirty_part = lax.psum_scatter(dirty, "tm", scatter_dimension=1, tiled=True)
    return (dirty_part, residual)


def solution(mesh):
    placed = (
        P(None, ("tile", "tm"), None),
        P(("tile", "tm"), None, None),
        P(("tile", "tm"), None, None),
        P(("tile", "tm"), None, None),
        P(("tile", "tm"), None),
        P(("tile", "tm")),
        P(("tile", "tm")),
    )
    return jax.shard_map(
        shards,
        mesh=mesh,
        in_specs=placed,
        out_specs=(P(None, ("tile", "tm"), None), P(("tile", "tm"), None, None)),
        check_vma=False,
    )
```

time: 1500 us -> 206 us (0.14); the launches traced: 1480 us -> 205 us
  local copies, waits for them, and re-layouts: 683 us -> 3.87 us
  loops' own time: 502 us -> 0 us
  Pallas kernels: 0 us -> 138 us
  other arithmetic: 126 us -> 2.53 us
  starting transfers between devices: 51.4 us -> 0.04 us
  matrix products: 34 us -> 0 us
  blocking collectives: 21.2 us -> 0 us
    another operation x2 -> x0, loops' own time: 502 us -> none  [the longest x1 501 us: add_patches(): return lax.fori_loop(0, subgrids.shape[0], add_one, total)]
    gather x385 -> x0, local copies, waits for them, and re-layouts: 342 us -> none
    dynamic_slice x256 -> x0, local copies, waits for them, and re-layouts: 151 us -> none  [add_one(): corner = (anchor, row_at[index], col_base[index])]
    dynamic_update_slice x128 -> x0, local copies, waits for them, and re-layouts: 146 us -> none  [add_one(): return lax.dynamic_update_slice(running, window + subgrids[index], corner)]
    pallas_call x0 -> x2, Pallas kernels: none -> 138 us  [the longest x1 128 us: shards(): pl.pallas_call(functools.partial(major_kernel, tiles, group, slots), out_...]
    add x129 -> x2, other arithmetic: 120 us -> 1.35 us  [the longest x1 0.68 us: shards(): wanted + 1]
    all_to_all x5 -> x0, starting transfers between devices: 51.1 us -> none  [the longest x1 14 us: shards(): lax.all_to_all(to_slots(row_offset), 'tile', split_axis=0, concat_axis=0,...]
    dot_general x3 -> x0, matrix products: 34 us -> none  [the longest x1 11.6 us: degrid_regrid(): jnp.einsum('scuj,svj->scuv', weighted, kern_wide, preferred_element_type=...]
  transfers between devices with their start and end apart: 7 -> 1, of which waited for: 4 -> 1; matrix products, arithmetic and copies ran while one was open for 27% -> 0% of each run, Pallas kernels for 0% -> 0%
where the time goes in v2:
time: 206 us; the launch traced here: 205 us
  Pallas kernels  138 us (67%)
  waiting for transfers between devices  46.4 us (23%)
  between operations  14.1 us (7%)
  local copies, waits for them, and re-layouts  3.87 us (2%)
  other arithmetic  2.53 us (1%)
    pallas_call x1, Pallas kernels, shards(): pl.pallas_call(functools.partial(major_kernel, tiles, group, slots), out_...  128 us
    reduce_scatter x1, waiting for transfers between devices, shards(): dirty_part = lax.psum_scatter(dirty, 'tm', scatter_dimension=1, tiled=True)  46.3 us
    pallas_call x1, Pallas kernels, shards(): pl.pallas_call(functools.partial(add_kernel, slots=slots), out_shape=jax....  10.3 us
  transfers between devices with their start and end apart: 1, of which 1 were waited for; matrix products, arithmetic and copies ran while one was open for 0% of the time, Pallas kernels for 0%

profile of v2, /device:TPU:6, one launch (start us, length us, event | category | flops | bytes accessed | tf_op | source)
XLA Modules:
  0.0 205.2 jit_solution(6781936882481928077)
XLA Ops:
  7.2 0.0 reduce-scatter.2.cloned.1.call-start
  7.2 0.9 convert_reduce_fusion
  8.1 0.7 multiply_add_fusion.pos_ref
  8.8 0.1 select_reduce_fusion.inv_ref
  8.9 0.1 fusion
  9.0 0.7 add_add_fusion
  9.6 0.1 multiply_reduce_fusion
  9.7 0.1 copy.10
  9.9 0.1 sub.7
  10.0 0.0 copy-start
  10.0 1.1 copy-done
  11.1 0.0 copy-start.1
  11.1 0.9 copy-done.1
  12.0 0.0 copy-start.2
  12.0 0.8 copy-done.2
  12.8 128.0 %major.1 = (bf16[64,2,2,32,128]{4,3,2,1,0:T(8,128)(2,1)S(1)}, f32[48,2,256]{2,1,0:T(2,128)S(1)}, s32[64,1,128]{2,1,0:T(1,128)S(1)}) custom-call(s32[128]{0:T(128)S(1)} %select_reduce_fusion.inv_ref, s32[48]{0:T(128)S(1)} %multiply_add_fusion.pos_ref, s32[64,1,128]{2,1,0:T(1,128)S(1)} %pad.4.req_ref, bf16[2,32,1024]{2,1,0:T(8,128)(2,1)S(1)} %copy-done.1, ...), custom_call_target="tpu_custom_call" | custom-call | tf_op jit(solution)/shard_map/major/pallas_call | solution.py:263
  140.9 0.1 slice_reduce_fusion
  140.9 0.1 reshape_squeeze.3.req_ref
  141.0 10.3 %add.39 = f32[2,256,1024]{2,1,0:T(8,128)} custom-call(s32[256]{0:T(256)S(1)} %reshape_squeeze.3.req_ref, bf16[64,2,2,32,128]{4,3,2,1,0:T(8,128)(2,1)S(1)} %get-tuple-element.6.subs), custom_call_target="tpu_custom_call" | custom-call | tf_op jit(solution)/shard_map/add/pallas_call | solution.py:300
  151.3 0.0 reduce-scatter.2.cloned.1.call-update
  151.3 46.3 %reduce-scatter.2.cloned.1.call-done = f32[2,32,1024]{2,1,0:T(8,128)} async-done(((f32[2,256,1024]{2,1,0:T(8,128)}), f32[2,32,1024]{2,1,0:T(8,128)}) %reduce-scatter.2.cloned.1.call-update) | async-done | bytes 262160 | tf_op jit(solution)/shard_map/reduce_scatter | solution.py:308
  197.7 0.6 copy.13
  (2 shorter events, 0.0 us)
Async XLA Ops:
  7.2 190.5 %reduce-scatter.2.cloned.1.call-start = ((), (), s32[]{:S(2)}) async-start(), calls=%async_computation.1 | async-start | bytes 2359296 | tf_op jit(solution)/shard_map/reduce_scatter | solution.py:308
  10.0 1.1 copy-start
  11.1 0.9 copy-start.1
  12.0 0.8 copy-start.2
Sparse Core Ops, SparseCore 0:
  151.4 46.1 reduce-scatter.1

commit v3 on v2

--- a/solution.py
+++ b/solution.py
@@ -11,18 +11,14 @@
 MESH = pl.DeviceIdType.MESH
 
 
-def corner(row, col, shape, sub_rows, sub_cols):
-    top = jnp.minimum(row // 8, (shape[0] - sub_rows) // 8 - 1) * 8
-    base = jnp.minimum(col // sub_cols, shape[1] // sub_cols - 2) * sub_cols
-    return pl.multiple_of(top, 8), row - top, pl.multiple_of(base, sub_cols), col - base
-
-
 def major_kernel(
     tiles, group, slots,
     inv_ref, pos_ref, req_ref, model_ref, rows_hbm, cols_hbm, vis_hbm,
-    back_ref, res_ref, asked,
-    panel, cells, asked_s, patch_out, patch_in, sub_out, rows_ref, cols_ref, vis_ref, res_slots,
+    out_ref, res_ref,
+    asked, panel, cells, asked_s, patch_out, patch_in, sub_out, back_ref, rows_ref, cols_ref, vis_ref, res_slots,
+    spread_ref, acc, sums,
     kern_sem, smem_sem, ask_send, ask_recv, ring_send, ring_recv, patch_send, patch_recv, back_send, back_recv,
+    sum_send, sum_recv,
 ):
     me = lax.axis_index("tile")
     tm = lax.axis_index("tm")
@@ -53,6 +49,13 @@
     def to_tile(src, dst, send, recv, peer, mine):
         return pltpu.make_async_remote_copy(
             src_ref=src.at[peer], dst_ref=dst.at[mine], send_sem=send.at[peer], recv_sem=recv.at[mine],
+            device_id=(peer, tm), device_id_type=MESH,
+        )
+
+    def give_back(c, peer, mine):
+        return pltpu.make_async_remote_copy(
+            src_ref=sub_out.at[c, peer], dst_ref=back_ref.at[c, mine],
+            send_sem=back_send.at[c, peer], recv_sem=back_recv.at[c, mine],
             device_id=(peer, tm), device_id_type=MESH,
         )
 
@@ -170,9 +173,12 @@
             sub = lax.dot_general(
                 weighted, cols, (((1,), (1,)), ((), ())), preferred_element_type=jnp.float32
             )
-            target[peer, s] = sub.astype(jnp.bfloat16).reshape(2, sub_rows, sub_cols)
+            sub = sub.astype(jnp.bfloat16).reshape(2, sub_rows, sub_cols)
+            for c in range(2):
+                target[c, peer, s] = sub[c]
 
     work(me, back_ref)
+    acc[...] = jnp.zeros_like(acc)
 
     @pl.loop(0, (tiles - 1) // width)
     def _(i):
@@ -182,46 +188,133 @@
         for peer in peers:
             work(peer, sub_out)
         for peer in peers:
-            to_tile(sub_out, back_ref, back_send, back_recv, peer, me).start()
+            give_back(0, peer, me).start()
+
+    @pl.loop(1, tiles)
+    def _(k):
+        give_back(1, lax.rem(me + tiles - k, tiles), me).start()
 
     @pl.loop(0, res_ref.shape[0], unroll=4)
     def _(b):
         res_ref[b] = res_slots[pos_ref[b]]
+
+    chunk = acc.shape[3]
+    halves = acc.shape[1]
+    tile_rows = acc.shape[2]
+
+    def sum_copy(c, h, way, step):
+        length = hops[way ^ h]
+        away = length - step
+        shard = lax.rem(tm - away + group, group) if way == 0 else lax.rem(tm + away, group)
+        rows = pl.ds(pl.multiple_of(shard * shard_rows, shard_rows), shard_rows)
+        src = acc.at[c, h, rows] if step == 0 else sums.at[c, h, way, step - 1]
+        copy = pltpu.make_async_remote_copy(
+            src_ref=src, dst_ref=sums.at[c, h, way, step],
+            send_sem=sum_send.at[c, h, way, step], recv_sem=sum_recv.at[c, h, way, step],
+            device_id=(me, left if way == 0 else right), device_id_type=MESH,
+        )
+        return copy, rows
+
+    chains = [(h, way) for h in range(halves) for way in range(2) if hops[way ^ h] > 0]
+
+    def sum_step(c, step):
+        for h, way in chains:
+            length = hops[way ^ h]
+            if step > 0 and step <= length:
+                sum_copy(c, h, way, step - 1)[0].wait_recv()
+            if step < length:
+                copy, rows = sum_copy(c, h, way, step)
+                if step > 0:
+                    sums[c, h, way, step - 1] += acc[c, h, rows]
+                copy.start()
+        if step == max(hops):
+            own = pl.ds(pl.multiple_of(tm * shard_rows, shard_rows), shard_rows)
+            for h in range(halves):
+                total = acc[c, h, own]
+                for way in range(2):
+                    if hops[way ^ h] > 0:
+                        total += sums[c, h, way, hops[way ^ h] - 1]
+                out_ref[c, :, h * chunk : (h + 1) * chunk] = total
+
+    batch = min(8, tiles)
+    turns = tiles // batch
+    lane = lax.broadcasted_iota(jnp.int32, (1, 128), 1)
+    grid_row = lax.broadcasted_iota(jnp.int32, (tile_rows, 128), 0)
+    place_gap = lax.broadcasted_iota(jnp.int32, (sub_cols, broad), 1) - lax.broadcasted_iota(
+        jnp.int32, (sub_cols, broad), 0
+    )
+    per = 128 // sub_rows
+    col_tiles = spread_ref.shape[1] // sub_cols
+
+    def add_batch(c, i):
+        starts = []
+        for w in range(batch):
+            k = i * batch + w
+            peer = lax.rem(me + k, tiles)
+
+            @pl.when(k > 0)
+            def _():
+                give_back(c, peer, peer).wait_recv()
+
+        for w in range(batch):
+            peer = lax.rem(me + i * batch + w, tiles)
+            for s in range(slots):
+                row = asked_s[peer, 0, 2 * s]
+                col = jnp.maximum(asked_s[peer, 0, 2 * s + 1], 0)
+                starts.append(jnp.where(row < 0, -4 * tile_rows, row))
+                base = jnp.minimum(lax.div(col, sub_cols), col_tiles - 2)
+                put = (place_gap == col - sub_cols * base).astype(jnp.float32).astype(jnp.bfloat16)
+                moved = jnp.dot(back_ref[c, peer, s], put, preferred_element_type=jnp.float32)
+                at = (w * slots + s) * sub_rows
+                where = jnp.broadcast_to(base, (sub_rows, sub_cols))
+                low, high = moved[:, :sub_cols], moved[:, sub_cols:]
+                for t in range(col_tiles):
+                    piece = jnp.where(where == t, low, jnp.where(where == t - 1, high, 0.0))
+                    spread_ref[at : at + sub_rows, t * sub_cols : (t + 1) * sub_cols] = piece.astype(jnp.bfloat16)
+        hot = []
+        for q in range(0, len(starts), per):
+            first = jnp.broadcast_to(starts[q + per - 1], (1, 128))
+            for r in range(per - 2, -1, -1):
+                first = jnp.where(lane < (r + 1) * sub_rows, starts[q + r], first)
+            first = first + lax.rem(lane, sub_rows)
+            hot.append((grid_row == first).astype(jnp.float32).astype(jnp.bfloat16))
+        hot = jnp.concatenate(hot, axis=1)
+        for h in range(halves):
+            for n in range(0, chunk, 256):
+                at = h * chunk + n
+                acc[c, h, :, n : n + 256] += jnp.dot(
+                    hot, spread_ref[:, at : at + 256], preferred_element_type=jnp.float32
+                )
+
+    @pl.loop(0, 2 * turns)
+    def _(j):
+        add_batch(j // turns, lax.rem(j, turns))
+        for step in range(max(hops)):
+
+            @pl.when(j == turns - 1 + step * turns // max(hops))
+            def _():
+                sum_step(0, step)
+
+    sum_step(1, 0)
+    sum_step(0, max(hops))
+    for step in range(max(hops)):
+        sum_step(1, step + 1)
 
     for c in range(2):
         for way in range(2):
             for step in range(hops[way]):
                 ring(way, step, c).wait_send()
+        for h, way in chains:
+            for step in range(hops[way ^ h]):
+                sum_copy(c, h, way, step)[0].wait_send()
 
     @pl.loop(1, tiles)
     def _(k):
         peer = lax.rem(me + k, tiles)
         to_tile(req_ref, asked, ask_send, ask_recv, peer, me).wait_send()
         to_tile(patch_out, patch_in, patch_send, patch_recv, peer, me).wait_send()
-        to_tile(sub_out, back_ref, back_send, back_recv, peer, me).wait_send()
-        to_tile(sub_out, back_ref, back_send, back_recv, peer, peer).wait_recv()
-
-
-def add_kernel(req_ref, subs, acc, *, slots):
-    tiles, sub_rows, sub_cols = subs.shape[0], subs.shape[3], subs.shape[4]
-    acc[...] = jnp.zeros_like(acc)
-
-    @pl.loop(0, tiles * slots)
-    def _(i):
-        row = req_ref[2 * i]
-        col = req_ref[2 * i + 1]
-
-        @pl.when(row >= 0)
-        def _():
-            top, down, base, right = corner(row, col, acc.shape[1:], sub_rows, sub_cols)
-            for c in range(2):
-                sub = subs[i // slots, lax.rem(i, slots), c].astype(jnp.float32)
-                window = jnp.concatenate([sub, jnp.zeros_like(sub)], axis=1)
-                window = pltpu.roll(window, right, 1)
-                window = jnp.concatenate([window, jnp.zeros((8, 2 * sub_cols), jnp.float32)], axis=0)
-                window = pltpu.roll(window, down, 0)
-                at = (c, pl.ds(top, sub_rows + 8), pl.ds(base, 2 * sub_cols))
-                acc[at] = acc[at] + window
+        for c in range(2):
+            give_back(c, peer, me).wait_send()
 
 
 def smem():
@@ -260,26 +353,32 @@
     pair = (tiles, slots, 2, sub_rows, sub_cols)
     hops = max(group // 2, 1)
     dma = pltpu.SemaphoreType.DMA
-    returned, residual, asked = pl.pallas_call(
+    back = (2, tiles, slots, sub_rows, sub_cols)
+    batch = min(8, tiles)
+    return pl.pallas_call(
         functools.partial(major_kernel, tiles, group, slots),
         out_shape=[
-            jax.ShapeDtypeStruct(pair, jnp.bfloat16),
+            jax.ShapeDtypeStruct((2, shard_rows, grid_cols), jnp.float32),
             jax.ShapeDtypeStruct((blocks, 2, vis_n), jnp.float32),
-            jax.ShapeDtypeStruct((tiles, 1, 128), jnp.int32),
         ],
         in_specs=[smem(), smem(), vmem(), vmem(), anywhere(), anywhere(), anywhere()],
-        out_specs=[vmem(), vmem(), vmem()],
+        out_specs=[vmem(), vmem()],
         scratch_shapes=[
+            pltpu.VMEM((tiles, 1, 128), jnp.int32),
             pltpu.VMEM((group, 2, shard_rows, grid_cols), jnp.bfloat16),
             pltpu.VMEM((2, tile_rows // 16, grid_cols // sub_cols, 16, sub_cols), jnp.bfloat16),
             pltpu.SMEM((tiles, 1, 128), jnp.int32),
             pltpu.VMEM(pair, jnp.bfloat16),
             pltpu.VMEM(pair, jnp.bfloat16),
-            pltpu.VMEM(pair, jnp.bfloat16),
+            pltpu.VMEM(back, jnp.bfloat16),
+            pltpu.VMEM(back, jnp.bfloat16),
             pltpu.VMEM(kern_rows.shape, jnp.bfloat16),
             pltpu.VMEM(kern_cols.shape, jnp.bfloat16),
             pltpu.VMEM(visibilities.shape, jnp.bfloat16),
             pltpu.VMEM((tiles * slots, 2, vis_n), jnp.float32),
+            pltpu.VMEM((batch * slots * sub_rows, grid_cols), jnp.bfloat16),
+            pltpu.VMEM((2, 2, tile_rows, grid_cols // 2), jnp.float32),
+            pltpu.VMEM((2, 2, 2, hops, shard_rows, grid_cols // 2), jnp.float32),
             dma((3,)),
             dma,
             dma((tiles,)),
@@ -288,25 +387,16 @@
             dma((2, hops, 2)),
             dma((tiles,)),
             dma((tiles,)),
-            dma((tiles,)),
-            dma((tiles,)),
+            dma((2, tiles)),
+            dma((2, tiles)),
+            dma((2, 2, 2, hops)),
+            dma((2, 2, 2, hops)),
         ],
         compiler_params=pltpu.CompilerParams(
             collective_id=0, has_side_effects=True, vmem_limit_bytes=VMEM_LIMIT
         ),
         name="major",
     )(inverse, place, request, model, kern_rows, kern_cols, visibilities)
-
-    dirty = pl.pallas_call(
-        functools.partial(add_kernel, slots=slots),
-        out_shape=jax.ShapeDtypeStruct((2, tile_rows, grid_cols), jnp.float32),
-        in_specs=[smem(), vmem()],
-        out_specs=vmem(),
-        compiler_params=pltpu.CompilerParams(vmem_limit_bytes=VMEM_LIMIT),
-        name="add",
-    )(asked[:, 0, : slots * 2].reshape(-1), returned)
-    dirty_part = lax.psum_scatter(dirty, "tm", scatter_dimension=1, tiled=True)
-    return (dirty_part, residual)
 
 
 def solution(mesh):

time: 206 us -> 161 us (0.78)
  waiting for transfers between devices: 46.4 us -> 0 us
  between operations: 14.1 us -> 0.67 us
  Pallas kernels: 138 us -> 150 us
  local copies, waits for them, and re-layouts: 3.87 us -> 6.28 us
    reduce_scatter x1 -> x0, waiting for transfers between devices: 46.3 us -> none  [shards(): dirty_part = lax.psum_scatter(dirty, 'tm', scatter_dimension=1, tiled=True)]
    pallas_call x1, Pallas kernels: 128 us -> 150 us  [shards(): pl.pallas_call(functools.partial(major_kernel, tiles, group, slots), out_...]
    pallas_call x1 -> x0, Pallas kernels: 10.3 us -> none  [shards(): pl.pallas_call(functools.partial(add_kernel, slots=slots), out_shape=jax....]
    unnamed x7 -> x10, local copies, waits for them, and re-layouts: 3.47 us -> 6.06 us
  transfers between devices with their start and end apart: 1 -> 0, of which waited for: 1 -> 0; matrix products, arithmetic and copies ran while one was open for 0% -> 0% of each run, Pallas kernels for 0% -> 0%
where the time goes in v3:
time: 161 us; the launch traced here: 159 us
  Pallas kernels  150 us (93%)
  local copies, waits for them, and re-layouts  6.28 us (4%)
  other arithmetic  2.52 us (2%)
    pallas_call x1, Pallas kernels, shards(): pl.pallas_call(functools.partial(major_kernel, tiles, group, slots), out_...  150 us
    unnamed x10, local copies, waits for them, and re-layouts  6.06 us

profile of v3, /device:TPU:6, one launch (start us, length us, event | category | flops | bytes accessed | tf_op | source)
XLA Modules:
  0.0 159.2 jit_solution(12342589905138699244)
XLA Ops:
  0.6 0.9 convert_reduce_fusion
  1.5 0.7 multiply_add_fusion.pos_ref
  2.2 0.1 select_reduce_fusion.inv_ref
  2.3 0.7 add_add_fusion
  3.0 0.1 fusion
  3.1 0.1 multiply_reduce_fusion
  3.2 0.1 copy.10
  3.3 0.1 sub.7
  3.4 0.0 copy-start
  3.4 1.9 %copy-done = bf16[48,128,256]{2,1,0:T(8,128)(2,1)S(1)} copy-done((bf16[48,128,256]{2,1,0:T(8,128)(2,1)S(1)}, bf16[48,128,256]{2,1,0:T(8,128)(2,1)}, u32[]{:S(2)}) %copy-start) | copy-done | bytes 3145752
  5.3 0.0 copy-start.1
  5.3 1.1 copy-done.1
  6.4 0.0 copy-start.2
  6.4 0.9 copy-done.2
  7.3 0.0 copy-start.3
  7.3 0.8 copy-done.3
  8.1 149.7 %major.1 = (f32[2,32,1024]{2,1,0:T(8,128)S(1)}, f32[48,2,256]{2,1,0:T(2,128)S(1)}) custom-call(s32[128]{0:T(128)S(1)} %select_reduce_fusion.inv_ref, s32[48]{0:T(128)S(1)} %multiply_add_fusion.pos_ref, s32[64,1,128]{2,1,0:T(1,128)S(1)} %pad.4.req_ref, bf16[2,32,1024]{2,1,0:T(8,128)(2,1)S(1)} %copy-done.2, bf16[48,32,256]{2,1,0:T(8,128)(2,1)S(1)} %copy-done.1, ...), custom_call_target="tpu_custom_call" | custom-call | tf_op jit(solution)/shard_map/major/pallas_call | solution.py:358
  157.9 0.7 copy.14
  158.6 0.6 copy.15
  (2 shorter events, 0.0 us)
Async XLA Ops:
  3.4 1.9 %copy-start = (bf16[48,128,256]{2,1,0:T(8,128)(2,1)S(1)}, bf16[48,128,256]{2,1,0:T(8,128)(2,1)}, u32[]{:S(2)}) copy-start(bf16[48,128,256]{2,1,0:T(8,128)(2,1)} %cols_hbm.1) | copy-start | bytes 9437188
  5.3 1.1 copy-start.1
  6.4 0.9 copy-start.2
  7.3 0.8 copy-start.3

commit v4 on v3

v4 whole, which is shorter than its diff:
```python
import functools

import jax
import jax.numpy as jnp
from jax import lax
from jax.experimental import pallas as pl
from jax.experimental.pallas import tpu as pltpu
from jax.sharding import PartitionSpec as P

VMEM_LIMIT = 48 * 1024 * 1024
MESH = pl.DeviceIdType.MESH


def tile_dims(tiles):
    return 8, (2 if tiles >= 16 else 1)


def major_kernel(
    tiles, group, slots,
    inv_ref, pos_ref, req_ref, model_ref, rows_hbm, cols_hbm, vis_hbm,
    out_ref, res_ref,
    asked, swapped, panel, cells, asked_s, patch_out, patch_in, sub_out, back_ref, rows_ref, cols_ref, vis_ref, res_slots,
    spread_ref, acc, sums, gift,
    kern_sem, smem_sem, ask_send, ask_recv, swap_send, swap_recv, strip_send, strip_recv, patch_send, patch_recv, back_send, back_recv,
    sum_send, sum_recv,
):
    me = lax.axis_index("tile")
    tm = lax.axis_index("tm")
    sub_rows, sub_cols = patch_in.shape[3], patch_in.shape[4]
    shard_rows = model_ref.shape[1]
    vis_n = rows_ref.shape[2]
    depth, cores = tile_dims(tiles)
    kind = lax.rem(tm // 2, 2)
    turn = 2 * lax.rem(tm, 2) - 1

    def plane(start, offset):
        return lax.rem(start + offset + group, group)

    mate, across, far = plane(tm, -turn), plane(tm, turn), plane(tm, 3 * turn)
    skip_to, skip_from = plane(tm, -2 * turn), plane(tm, 2 * turn)
    passed = (far, across, skip_from)
    mates = (plane(mate, -3 * turn), plane(mate, -turn), plane(mate, -2 * turn))
    x, z, core = me // (depth * cores), lax.rem(me // cores, depth), lax.rem(me, cores)
    opposite = (x * depth + lax.rem(z + depth // 2, depth)) * cores + core
    per_z = tiles // depth
    near = depth // 2 + 1
    own = (near // 2) * per_z

    def partner(i, flip=False):
        k = lax.rem(own + i, tiles)
        other = k // (near * per_z)
        rest = k - other * near * per_z
        dz, dx, dc = rest // per_z, lax.rem(rest, per_z) // cores, lax.rem(rest, cores)
        back_dz, back_dx = near - 1 - 2 * other - dz, lax.rem(per_z // cores - dx, per_z // cores)
        back = other * near * per_z + back_dz * per_z + back_dx * cores + dc
        if flip:
            dz, dx, k, back = back_dz, back_dx, back, k
        there = (
            lax.rem(x + dx, per_z // cores) * depth + lax.rem(z + dz - near // 2 + other + depth, depth)
        ) * cores + lax.rem(core + dc, cores)
        return (there, jnp.where(other == 1, across, tm)), k, back

    width = 3 if (tiles - 1) % 3 == 0 else 1

    loads = [
        pltpu.make_async_copy(src, dst, kern_sem.at[i])
        for i, (src, dst) in enumerate(((rows_hbm, rows_ref), (cols_hbm, cols_ref), (vis_hbm, vis_ref)))
    ]
    for load in loads:
        load.start()

    barrier = pltpu.get_barrier_semaphore()

    @pl.loop(1, tiles)
    def _(i):
        pl.semaphore_signal(barrier, inc=1, device_id=partner(i)[0], device_id_type=MESH)

    others = ((me, mate), (me, far), (me, skip_to), (me, skip_from), (opposite, tm))
    for other in others:
        pl.semaphore_signal(barrier, inc=1, device_id=other, device_id_type=MESH)
    pl.semaphore_wait(barrier, tiles - 1 + len(others))

    def to_tile(src, dst, send, recv, i):
        device, here, there = partner(i)
        return pltpu.make_async_remote_copy(
            src_ref=src.at[here], dst_ref=dst.at[there], send_sem=send.at[here], recv_sem=recv.at[there],
            device_id=device, device_id_type=MESH,
        )

    def from_tile(dst, send, recv, i):
        device, here, there = partner(i, True)
        return pltpu.make_async_remote_copy(
            src_ref=dst.at[here], dst_ref=dst.at[here], send_sem=send.at[here], recv_sem=recv.at[here],
            device_id=device, device_id_type=MESH,
        )

    def give_back(c, i):
        device, here, there = partner(i, True)
        return pltpu.make_async_remote_copy(
            src_ref=sub_out.at[c, here], dst_ref=back_ref.at[c, there],
            send_sem=back_send.at[c, here], recv_sem=back_recv.at[c, there],
            device_id=device, device_id_type=MESH,
        )

    def returned(c, i):
        device, here, there = partner(i)
        return pltpu.make_async_remote_copy(
            src_ref=back_ref.at[c, here], dst_ref=back_ref.at[c, here],
            send_sem=back_send.at[c, here], recv_sem=back_recv.at[c, here],
            device_id=device, device_id_type=MESH,
        )

    def swap(c):
        return pltpu.make_async_remote_copy(
            src_ref=model_ref.at[c], dst_ref=swapped.at[c], send_sem=swap_send.at[c], recv_sem=swap_recv.at[c],
            device_id=(opposite, tm), device_id_type=MESH,
        )

    def strip(src, index, label, shard, c, to):
        return pltpu.make_async_remote_copy(
            src_ref=src, dst_ref=panel.at[shard, c],
            send_sem=strip_send.at[index, c], recv_sem=strip_recv.at[label, c],
            device_id=(me, to), device_id_type=MESH,
        )

    def outgoing(index, c):
        src = model_ref.at[c] if index < 2 else swapped.at[c]
        same = kind == (0 if index < 2 else 1)
        step = index % 2
        label = jnp.where(same, step, 2 + step)
        to = jnp.where(same, (mate, far)[step], (across, skip_to)[step])
        return strip(src, index, label, tm, c, to)

    def passing(f, c):
        return strip(panel.at[passed[f], c], 4 + f, 4 + f, passed[f], c, mate)

    for c in range(2):
        swap(c).start()
        for index in range(2):
            outgoing(index, c).start()

    @pl.loop(1, tiles)
    def _(i):
        to_tile(req_ref, asked, ask_send, ask_recv, i).start()

    asked[own] = req_ref[own]

    def spread(c, shard, values):
        for h in range(shard_rows // 16):
            for t in range(values.shape[1] // sub_cols):
                cells[c, shard * (shard_rows // 16) + h, t] = values[
                    h * 16 : (h + 1) * 16, t * sub_cols : (t + 1) * sub_cols
                ]

    for c in range(2):
        swap(c).wait_recv()
        for index in range(2, 4):
            outgoing(index, c).start()
    for c in range(2):
        spread(c, tm, jnp.where(kind == 0, model_ref[c], swapped[c]))
    for c in range(2):
        for f in range(3):
            strip(panel.at[passed[f], c], 4 + f, 1 + f, passed[f], c, mate).wait_recv()
            passing(f, c).start()
            spread(c, passed[f], panel[passed[f], c])
    for c in range(2):
        strip(panel.at[mate, c], 0, 0, mate, c, mate).wait_recv()
        spread(c, mate, panel[mate, c])
        for f in range(3):
            strip(panel.at[mates[f], c], 4 + f, 4 + f, mates[f], c, mate).wait_recv()
            spread(c, mates[f], panel[mates[f], c])

    @pl.loop(1, tiles)
    def _(i):
        from_tile(asked, ask_send, ask_recv, i).wait_recv()

    to_smem = pltpu.make_async_copy(asked, asked_s, smem_sem)
    to_smem.start()
    to_smem.wait()

    tall, broad = sub_rows + 16, 2 * sub_cols
    row_gap = lax.broadcasted_iota(jnp.int32, (sub_rows, tall), 1) - lax.broadcasted_iota(
        jnp.int32, (sub_rows, tall), 0
    )
    col_gap = lax.broadcasted_iota(jnp.int32, (broad, sub_cols), 0) - lax.broadcasted_iota(
        jnp.int32, (broad, sub_cols), 1
    )

    def cut(peer, target):
        for s in range(slots):
            row = jnp.maximum(asked_s[peer, 0, 2 * s], 0)
            col = jnp.maximum(asked_s[peer, 0, 2 * s + 1], 0)
            top = jnp.minimum(lax.div(row, 16), cells.shape[1] - tall // 16)
            base = jnp.minimum(lax.div(col, sub_cols), cells.shape[2] - 2)
            window = jnp.concatenate(
                [
                    jnp.concatenate([cells[c, top + i, base + j] for c in range(2) for j in range(2)], axis=1)
                    for i in range(tall // 16)
                ],
                axis=0,
            )
            pick_rows = (row_gap == row - 16 * top).astype(jnp.float32).astype(jnp.bfloat16)
            pick_cols = (col_gap == col - sub_cols * base).astype(jnp.float32).astype(jnp.bfloat16)
            window = jnp.dot(pick_rows, window, preferred_element_type=jnp.float32).astype(jnp.bfloat16)
            window = jnp.concatenate([window[:, :broad], window[:, broad:]], axis=0)
            window = jnp.dot(window, pick_cols, preferred_element_type=jnp.float32).astype(jnp.bfloat16)
            target[peer, s] = window.reshape(2, sub_rows, sub_cols)

    @pl.loop(0, (tiles - 1) // width)
    def _(i):
        turns_here = [1 + i * width + w for w in range(width)]
        for t in turns_here:
            cut(partner(t)[1], patch_out)
        for t in turns_here:
            to_tile(patch_out, patch_in, patch_send, patch_recv, t).start()

    cut(own, patch_in)
    for load in loads:
        load.wait()

    def work(peer, target):
        for s in range(slots):
            b = inv_ref[peer * slots + s]
            patch = patch_in[peer, s].reshape(2 * sub_rows, sub_cols)
            cols = cols_ref[b]
            sampled = jnp.dot(patch, cols, preferred_element_type=jnp.float32)
            weights = rows_ref[b].astype(jnp.float32)
            sampled = sampled.reshape(2, sub_rows, vis_n)
            predicted = jnp.sum(weights[None] * sampled, axis=1)
            residual = vis_ref[b].astype(jnp.float32) - predicted
            res_slots[peer * slots + s] = residual
            weighted = (weights[None] * residual[:, None, :]).astype(jnp.bfloat16)
            weighted = weighted.reshape(2 * sub_rows, vis_n)
            sub = lax.dot_general(
                weighted, cols, (((1,), (1,)), ((), ())), preferred_element_type=jnp.float32
            )
            sub = sub.astype(jnp.bfloat16).reshape(2, sub_rows, sub_cols)
            for c in range(2):
                target[c, peer, s] = sub[c]

    work(own, back_ref)
    acc[...] = jnp.zeros_like(acc)

    @pl.loop(0, (tiles - 1) // width)
    def _(i):
        turns_here = [1 + i * width + w for w in range(width)]
        for t in turns_here:
            from_tile(patch_in, patch_send, patch_recv, t).wait_recv()
        for t in turns_here:
            work(partner(t, True)[1], sub_out)
        for t in turns_here:
            give_back(0, t).start()

    @pl.loop(1, tiles)
    def _(i):
        give_back(1, i).start()

    @pl.loop(0, res_ref.shape[0], unroll=4)
    def _(b):
        res_ref[b] = res_slots[pos_ref[b]]

    chunk = acc.shape[3]
    halves = acc.shape[1]
    tile_rows = acc.shape[2]

    def rows_of(shard):
        return pl.ds(pl.multiple_of(shard * shard_rows, shard_rows), shard_rows)

    def sum_copy(c, h, index):
        if index in (0, 4, 5, 6):
            src, device = acc.at[c, h, rows_of(mate if index == 0 else mates[index - 4])], (me, mate)
        elif index < 4:
            src, device = sums.at[c, h, 3 + index], (me, passed[index - 1])
        else:
            src, device = gift.at[c, h], (opposite, tm)
        return pltpu.make_async_remote_copy(
            src_ref=src, dst_ref=sums.at[c, h, index],
            send_sem=sum_send.at[c, h, index], recv_sem=sum_recv.at[c, h, index],
            device_id=device, device_id_type=MESH,
        )

    def sum_step(c, step):
        for h in range(halves):
            cols = slice(h * chunk, (h + 1) * chunk)
            if step == 0:
                for index in (4, 5, 6, 0):
                    sum_copy(c, h, index).start()
            elif step == 1:
                for f in range(3):
                    sum_copy(c, h, 4 + f).wait_recv()
                    sums[c, h, 4 + f] += acc[c, h, rows_of(passed[f])]
                    sum_copy(c, h, 1 + f).start()
            elif step == 2:
                for index in range(4):
                    sum_copy(c, h, index).wait_recv()
                alike = acc[c, h, rows_of(tm)] + sums[c, h, 0] + sums[c, h, 1]
                unlike = sums[c, h, 2] + sums[c, h, 3]
                gift[c, h] = jnp.where(kind == 0, unlike, alike)
                sum_copy(c, h, 7).start()
                out_ref[c, :, cols] = jnp.where(kind == 0, alike, unlike)
            else:
                sum_copy(c, h, 7).wait_recv()
                out_ref[c, :, cols] += sums[c, h, 7]

    batch = min(8, tiles)
    turns = tiles // batch
    lane = lax.broadcasted_iota(jnp.int32, (1, 128), 1)
    grid_row = lax.broadcasted_iota(jnp.int32, (tile_rows, 128), 0)
    place_gap = lax.broadcasted_iota(jnp.int32, (sub_cols, broad), 1) - lax.broadcasted_iota(
        jnp.int32, (sub_cols, broad), 0
    )
    per = 128 // sub_rows
    col_tiles = spread_ref.shape[1] // sub_cols

    def add_batch(c, i):
        starts = []
        for w in range(batch):
            t = i * batch + w

            @pl.when(t > 0)
            def _():
                returned(c, t).wait_recv()

        for w in range(batch):
            peer = partner(i * batch + w)[1]
            for s in range(slots):
                row = asked_s[peer, 0, 2 * s]
                col = jnp.maximum(asked_s[peer, 0, 2 * s + 1], 0)
                starts.append(jnp.where(row < 0, -4 * tile_rows, row))
                base = jnp.minimum(lax.div(col, sub_cols), col_tiles - 2)
                put = (place_gap == col - sub_cols * base).astype(jnp.float32).astype(jnp.bfloat16)
                moved = jnp.dot(back_ref[c, peer, s], put, preferred_element_type=jnp.float32)
                at = (w * slots + s) * sub_rows
                where = jnp.broadcast_to(base, (sub_rows, sub_cols))
                low, high = moved[:, :sub_cols], moved[:, sub_cols:]
                for t in range(col_tiles):
                    piece = jnp.where(where == t, low, jnp.where(where == t - 1, high, 0.0))
                    spread_ref[at : at + sub_rows, t * sub_cols : (t + 1) * sub_cols] = piece.astype(jnp.bfloat16)
        hot = []
        for q in range(0, len(starts), per):
            first = jnp.broadcast_to(starts[q + per - 1], (1, 128))
            for r in range(per - 2, -1, -1):
                first = jnp.where(lane < (r + 1) * sub_rows, starts[q + r], first)
            first = first + lax.rem(lane, sub_rows)
            hot.append((grid_row == first).astype(jnp.float32).astype(jnp.bfloat16))
        hot = jnp.concatenate(hot, axis=1)
        for h in range(halves):
            for n in range(0, chunk, 256):
                at = h * chunk + n
                acc[c, h, :, n : n + 256] += jnp.dot(
                    hot, spread_ref[:, at : at + 256], preferred_element_type=jnp.float32
                )

    @pl.loop(0, 2 * turns)
    def _(j):
        add_batch(j // turns, lax.rem(j, turns))
        for step in range(4):

            @pl.when(j == turns - 1 + step * turns // 4)
            def _():
                sum_step(0, step)

    for step in range(4):
        sum_step(1, step)

    for c in range(2):
        swap(c).wait_send()
        for index in range(4):
            outgoing(index, c).wait_send()
        for f in range(3):
            passing(f, c).wait_send()
        for h in range(halves):
            for index in range(8):
                sum_copy(c, h, index).wait_send()

    @pl.loop(1, tiles)
    def _(i):
        to_tile(req_ref, asked, ask_send, ask_recv, i).wait_send()
        to_tile(patch_out, patch_in, patch_send, patch_recv, i).wait_send()
        for c in range(2):
            give_back(c, i).wait_send()


def smem():
    return pl.BlockSpec(memory_space=pltpu.SMEM)


def vmem():
    return pl.BlockSpec(memory_space=pltpu.VMEM)


def anywhere():
    return pl.BlockSpec(memory_space=pl.ANY)


def shards(model, kern_rows, kern_cols, visibilities, owner_tile, row_offset, col_offset):
    tiles = lax.axis_size("tile")
    group = lax.axis_size("tm")
    blocks = owner_tile.shape[0]
    slots = (blocks + tiles - 1) // tiles + 1
    sub_rows = kern_rows.shape[1]
    sub_cols = kern_cols.shape[1]
    vis_n = kern_rows.shape[2]
    shard_rows, grid_cols = model.shape[1:]
    tile_rows = group * shard_rows

    owners = owner_tile[:, 0]
    ids = jnp.arange(blocks, dtype=jnp.int32)
    earlier = (owners[:, None] == owners[None, :]) & (ids[None, :] < ids[:, None])
    depth, cores = tile_dims(tiles)
    near = depth // 2 + 1
    per_z = tiles // depth
    me = lax.axis_index("tile")
    kind = lax.rem(lax.axis_index("tm") // 2, 2)
    to_x = lax.rem(owners // (depth * cores) - me // (depth * cores) + per_z, per_z // cores)
    to_core = lax.rem(lax.rem(owners, cores) - lax.rem(me, cores) + cores, cores)
    to_z = lax.rem(
        lax.rem(owners // cores, depth) - lax.rem(me // cores, depth) + near // 2 + (4 - kind) * (depth // 2), depth
    )
    other = (to_z >= near).astype(jnp.int32)
    to_z = to_z - other * near
    at = (other * near + to_z) * per_z + to_x * cores + to_core
    place = at * slots + jnp.sum(earlier.astype(jnp.int32), axis=1)
    hot = (place[None, :] == jnp.arange(tiles * slots, dtype=jnp.int32)[:, None]).astype(jnp.int32)
    inverse = jnp.sum(hot * ids[None, :], axis=1)
    wanted = jnp.stack([row_offset, col_offset], axis=0)
    request = (jnp.sum(hot[:, None, :] * (wanted + 1)[None], axis=2) - 1).reshape(tiles, 1, slots * 2)
    request = jnp.pad(request, ((0, 0), (0, 0), (0, 128 - slots * 2)))

    pair = (tiles, slots, 2, sub_rows, sub_cols)
    dma = pltpu.SemaphoreType.DMA
    back = (2, tiles, slots, sub_rows, sub_cols)
    batch = min(8, tiles)
    return pl.pallas_call(
        functools.partial(major_kernel, tiles, group, slots),
        out_shape=[
            jax.ShapeDtypeStruct((2, shard_rows, grid_cols), jnp.float32),
            jax.ShapeDtypeStruct((blocks, 2, vis_n), jnp.float32),
        ],
        in_specs=[smem(), smem(), vmem(), vmem(), anywhere(), anywhere(), anywhere()],
        out_specs=[vmem(), vmem()],
        scratch_shapes=[
            pltpu.VMEM((tiles, 1, 128), jnp.int32),
            pltpu.VMEM((2, shard_rows, grid_cols), jnp.bfloat16),
            pltpu.VMEM((group, 2, shard_rows, grid_cols), jnp.bfloat16),
            pltpu.VMEM((2, tile_rows // 16, grid_cols // sub_cols, 16, sub_cols), jnp.bfloat16),
            pltpu.SMEM((tiles, 1, 128), jnp.int32),
            pltpu.VMEM(pair, jnp.bfloat16),
            pltpu.VMEM(pair, jnp.bfloat16),
            pltpu.VMEM(back, jnp.bfloat16),
            pltpu.VMEM(back, jnp.bfloat16),
            pltpu.VMEM(kern_rows.shape, jnp.bfloat16),
            pltpu.VMEM(kern_cols.shape, jnp.bfloat16),
            pltpu.VMEM(visibilities.shape, jnp.bfloat16),
            pltpu.VMEM((tiles * slots, 2, vis_n), jnp.float32),
            pltpu.VMEM((batch * slots * sub_rows, grid_cols), jnp.bfloat16),
            pltpu.VMEM((2, 2, tile_rows, grid_cols // 2), jnp.float32),
            pltpu.VMEM((2, 2, 8, shard_rows, grid_cols // 2), jnp.float32),
            pltpu.VMEM((2, 2, shard_rows, grid_cols // 2), jnp.float32),
            dma((3,)),
            dma,
            dma((tiles,)),
            dma((tiles,)),
            dma((2,)),
            dma((2,)),
            dma((7, 2)),
            dma((7, 2)),
            dma((tiles,)),
            dma((tiles,)),
            dma((2, tiles)),
            dma((2, tiles)),
            dma((2, 2, 8)),
            dma((2, 2, 8)),
        ],
        compiler_params=pltpu.CompilerParams(
            collective_id=0, has_side_effects=True, vmem_limit_bytes=VMEM_LIMIT
        ),
        name="major",
    )(inverse, place, request, model, kern_rows, kern_cols, visibilities)


def solution(mesh):
    placed = (
        P(None, ("tile", "tm"), None),
        P(("tile", "tm"), None, None),
        P(("tile", "tm"), None, None),
        P(("tile", "tm"), None, None),
        P(("tile", "tm"), None),
        P(("tile", "tm")),
        P(("tile", "tm")),
    )
    return jax.shard_map(
        shards,
        mesh=mesh,
        in_specs=placed,
        out_specs=(P(None, ("tile", "tm"), None), P(("tile", "tm"), None, None)),
        check_vma=False,
    )
```

time: 161 us -> 170 us (1.056)
  the two profiles are of different devices: /device:TPU:6 before, /device:TPU:70 now
where the time goes in v4:
time: 170 us
  Pallas kernels  160 us (94%)
  local copies, waits for them, and re-layouts  6.28 us (4%)
  other arithmetic  2.55 us (1%)
    pallas_call x1, Pallas kernels, shards(): pl.pallas_call(functools.partial(major_kernel, tiles, group, slots), out_...  160 us
    unnamed x10, local copies, waits for them, and re-layouts  6.06 us

profile of v4, /device:TPU:70, one launch (start us, length us, event | category | flops | bytes accessed | tf_op | source)
XLA Modules:
  0.0 169.8 jit_solution(16589587409571071414)
XLA Ops:
  0.7 0.9 convert_reduce_fusion
  1.6 0.7 multiply_add_fusion.pos_ref
  2.3 0.1 select_reduce_fusion.inv_ref
  2.4 0.7 add_add_fusion
  3.1 0.1 fusion
  3.1 0.1 multiply_reduce_fusion
  3.2 0.1 copy.10
  3.3 0.1 sub.73
  3.5 0.0 copy-start
  3.5 1.9 %copy-done = bf16[48,128,256]{2,1,0:T(8,128)(2,1)S(1)} copy-done((bf16[48,128,256]{2,1,0:T(8,128)(2,1)S(1)}, bf16[48,128,256]{2,1,0:T(8,128)(2,1)}, u32[]{:S(2)}) %copy-start) | copy-done | bytes 3145752
  5.4 0.0 copy-start.1
  5.4 1.1 copy-done.1
  6.5 0.0 copy-start.2
  6.5 0.9 copy-done.2
  7.4 0.0 copy-start.3
  7.4 0.8 copy-done.3
  8.2 160.3 %major.1 = (f32[2,32,1024]{2,1,0:T(8,128)S(1)}, f32[48,2,256]{2,1,0:T(2,128)S(1)}) custom-call(s32[128]{0:T(128)S(1)} %select_reduce_fusion.inv_ref, s32[48]{0:T(128)S(1)} %multiply_add_fusion.pos_ref, s32[64,1,128]{2,1,0:T(1,128)S(1)} %pad.4.req_ref, bf16[2,32,1024]{2,1,0:T(8,128)(2,1)S(1)} %copy-done.2, bf16[48,32,256]{2,1,0:T(8,128)(2,1)S(1)} %copy-done.1, ...), custom_call_target="tpu_custom_call" | custom-call | tf_op jit(solution)/shard_map/major/pallas_call | solution.py:434
  168.5 0.7 copy.14
  169.2 0.6 copy.15
  (2 shorter events, 0.0 us)
Async XLA Ops:
  3.5 1.9 %copy-start = (bf16[48,128,256]{2,1,0:T(8,128)(2,1)S(1)}, bf16[48,128,256]{2,1,0:T(8,128)(2,1)}, u32[]{:S(2)}) copy-start(bf16[48,128,256]{2,1,0:T(8,128)(2,1)} %cols_hbm.1) | copy-start | bytes 9437188
  5.4 1.1 copy-start.1
  6.5 0.9 copy-start.2
  7.4 0.8 copy-start.3

commit v5 on v3

--- a/solution.py
+++ b/solution.py
@@ -7,27 +7,36 @@
 from jax.experimental.pallas import tpu as pltpu
 from jax.sharding import PartitionSpec as P
 
-VMEM_LIMIT = 48 * 1024 * 1024
+VMEM_LIMIT = 63 * 1024 * 1024
 MESH = pl.DeviceIdType.MESH
 
 
 def major_kernel(
     tiles, group, slots,
-    inv_ref, pos_ref, req_ref, model_ref, rows_hbm, cols_hbm, vis_hbm,
+    owner_hbm, row_hbm, col_hbm, model_hbm, rows_hbm, cols_hbm, vis_hbm,
     out_ref, res_ref,
-    asked, panel, cells, asked_s, patch_out, patch_in, sub_out, back_ref, rows_ref, cols_ref, vis_ref, res_slots,
+    wanted, model_ref, req_ref, pos_v, req_s, pos_s, asked, panel, cells, asked_s, patch_out, patch_in, sub_out, back_ref, rows_ref, cols_ref, vis_ref, res_slots,
     spread_ref, acc, sums,
-    kern_sem, smem_sem, ask_send, ask_recv, ring_send, ring_recv, patch_send, patch_recv, back_send, back_recv,
+    kern_sem, want_sem, smem_sem, ask_send, ask_recv, ring_send, ring_recv, patch_send, patch_recv, back_send, back_recv,
     sum_send, sum_recv,
 ):
     me = lax.axis_index("tile")
     tm = lax.axis_index("tm")
+    blocks = res_ref.shape[0]
     sub_rows, sub_cols = patch_in.shape[3], patch_in.shape[4]
     shard_rows = model_ref.shape[1]
     vis_n = rows_ref.shape[2]
     right, left = lax.rem(tm + 1, group), lax.rem(tm + group - 1, group)
     width = 3 if (tiles - 1) % 3 == 0 else 1
 
+    first = [
+        pltpu.make_async_copy(src, dst, want_sem.at[i])
+        for i, (src, dst) in enumerate(
+            ((owner_hbm, wanted.at[0]), (row_hbm, wanted.at[1]), (col_hbm, wanted.at[2]), (model_hbm, model_ref))
+        )
+    ]
+    for load in first:
+        load.start()
     loads = [
         pltpu.make_async_copy(src, dst, kern_sem.at[i])
         for i, (src, dst) in enumerate(((rows_hbm, rows_ref), (cols_hbm, cols_ref), (vis_hbm, vis_ref)))
@@ -44,6 +53,31 @@
     near = [right, left] if group > 2 else [right]
     for other in near:
         pl.semaphore_signal(barrier, inc=1, device_id=(me, other), device_id_type=MESH)
+    for load in first:
+        load.wait()
+    owner, row_at, col_at = wanted[0], wanted[1], wanted[2]
+    ids = lax.broadcasted_iota(jnp.int32, (1, blocks), 1)
+    down = lax.broadcasted_iota(jnp.int32, (blocks, blocks), 0)
+    along = lax.broadcasted_iota(jnp.int32, (blocks, blocks), 1)
+    owner_down = jnp.sum(jnp.where(down == along, owner, 0), axis=1, keepdims=True)
+    earlier = jnp.where((owner_down == owner) & (down < along), 1, 0)
+    place = owner * slots + jnp.sum(earlier, axis=0, keepdims=True)
+    lanes = lax.broadcasted_iota(jnp.int32, (tiles, 128), 1)
+    tile_at = lax.broadcasted_iota(jnp.int32, (tiles, blocks), 0) * slots
+    request = jnp.zeros((tiles, 128), jnp.int32)
+    for s in range(slots):
+        hot = tile_at + s == place
+        for lane_at, value in ((2 * s, row_at + 1), (2 * s + 1, col_at + 1), (2 * slots + s, ids + 1)):
+            found = jnp.sum(jnp.where(hot, value, 0), axis=1, keepdims=True) - 1
+            request = jnp.where(lanes == lane_at, found, request)
+    req_ref[...] = request.reshape(tiles, 1, 128)
+    pos_v[...] = jnp.concatenate([place, jnp.zeros((1, 128 - blocks), jnp.int32)], axis=1)
+    lists = [
+        pltpu.make_async_copy(src, dst, want_sem.at[4 + i])
+        for i, (src, dst) in enumerate(((req_ref, req_s), (pos_v, pos_s)))
+    ]
+    for load in lists:
+        load.start()
     pl.semaphore_wait(barrier, tiles - 1 + len(near))
 
     def to_tile(src, dst, send, recv, peer, mine):
@@ -154,12 +188,12 @@
             to_tile(patch_out, patch_in, patch_send, patch_recv, peer, me).start()
 
     cut(me, patch_in)
-    for load in loads:
+    for load in loads + lists:
         load.wait()
 
     def work(peer, target):
         for s in range(slots):
-            b = inv_ref[peer * slots + s]
+            b = jnp.maximum(req_s[peer, 0, 2 * slots + s], 0)
             patch = patch_in[peer, s].reshape(2 * sub_rows, sub_cols)
             cols = cols_ref[b]
             sampled = jnp.dot(patch, cols, preferred_element_type=jnp.float32)
@@ -196,7 +230,7 @@
 
     @pl.loop(0, res_ref.shape[0], unroll=4)
     def _(b):
-        res_ref[b] = res_slots[pos_ref[b]]
+        res_ref[b] = res_slots[pos_s[0, b]]
 
     chunk = acc.shape[3]
     halves = acc.shape[1]
@@ -340,16 +374,6 @@
     shard_rows, grid_cols = model.shape[1:]
     tile_rows = group * shard_rows
 
-    owners = owner_tile[:, 0]
-    ids = jnp.arange(blocks, dtype=jnp.int32)
-    earlier = (owners[:, None] == owners[None, :]) & (ids[None, :] < ids[:, None])
-    place = owners * slots + jnp.sum(earlier.astype(jnp.int32), axis=1)
-    hot = (place[None, :] == jnp.arange(tiles * slots, dtype=jnp.int32)[:, None]).astype(jnp.int32)
-    inverse = jnp.sum(hot * ids[None, :], axis=1)
-    wanted = jnp.stack([row_offset, col_offset], axis=0)
-    request = (jnp.sum(hot[:, None, :] * (wanted + 1)[None], axis=2) - 1).reshape(tiles, 1, slots * 2)
-    request = jnp.pad(request, ((0, 0), (0, 0), (0, 128 - slots * 2)))
-
     pair = (tiles, slots, 2, sub_rows, sub_cols)
     hops = max(group // 2, 1)
     dma = pltpu.SemaphoreType.DMA
@@ -361,9 +385,15 @@
             jax.ShapeDtypeStruct((2, shard_rows, grid_cols), jnp.float32),
             jax.ShapeDtypeStruct((blocks, 2, vis_n), jnp.float32),
         ],
-        in_specs=[smem(), smem(), vmem(), vmem(), anywhere(), anywhere(), anywhere()],
+        in_specs=[anywhere()] * 7,
         out_specs=[vmem(), vmem()],
         scratch_shapes=[
+            pltpu.VMEM((3, 1, blocks), jnp.int32),
+            pltpu.VMEM(model.shape, jnp.bfloat16),
+            pltpu.VMEM((tiles, 1, 128), jnp.int32),
+            pltpu.VMEM((1, 128), jnp.int32),
+            pltpu.SMEM((tiles, 1, 128), jnp.int32),
+            pltpu.SMEM((1, 128), jnp.int32),
             pltpu.VMEM((tiles, 1, 128), jnp.int32),
             pltpu.VMEM((group, 2, shard_rows, grid_cols), jnp.bfloat16),
             pltpu.VMEM((2, tile_rows // 16, grid_cols // sub_cols, 16, sub_cols), jnp.bfloat16),
@@ -380,6 +410,7 @@
             pltpu.VMEM((2, 2, tile_rows, grid_cols // 2), jnp.float32),
             pltpu.VMEM((2, 2, 2, hops, shard_rows, grid_cols // 2), jnp.float32),
             dma((3,)),
+            dma((6,)),
             dma,
             dma((tiles,)),
             dma((tiles,)),
@@ -396,7 +427,10 @@
             collective_id=0, has_side_effects=True, vmem_limit_bytes=VMEM_LIMIT
         ),
         name="major",
-    )(inverse, place, request, model, kern_rows, kern_cols, visibilities)
+    )(
+        owner_tile.reshape(1, blocks), row_offset.reshape(1, blocks), col_offset.reshape(1, blocks),
+        model, kern_rows, kern_cols, visibilities,
+    )
 
 
 def solution(mesh):

time: 161 us -> 155 us (0.963)
  local copies, waits for them, and re-layouts: 6.28 us -> 3.21 us
  other arithmetic: 2.52 us -> 0 us
    unnamed x10 -> x2, local copies, waits for them, and re-layouts: 6.06 us -> 3.21 us
where the time goes in v5:
time: 155 us; the launch traced here: 153 us
  Pallas kernels  149 us (96%)
  local copies, waits for them, and re-layouts  3.21 us (2%)
    pallas_call x1, Pallas kernels, shards(): pl.pallas_call(functools.partial(major_kernel, tiles, group, slots), out_...  149 us
    unnamed x2, local copies, waits for them, and re-layouts  3.21 us

profile of v5, /device:TPU:6, one launch (start us, length us, event | category | flops | bytes accessed | tf_op | source)
XLA Modules:
  0.0 153.2 jit_solution(7419463878239917124)
XLA Ops:
  0.6 149.4 %major.1 = (f32[2,32,1024]{2,1,0:T(8,128)}, f32[48,2,256]{2,1,0:T(2,128)}) custom-call(s32[1,48]{1,0:T(1,128)} %bitcast.3, s32[1,48]{1,0:T(1,128)} %bitcast.4, s32[1,48]{1,0:T(1,128)} %bitcast.5, bf16[2,32,1024]{2,1,0:T(8,128)(2,1)} %model_hbm.1, bf16[48,32,256]{2,1,0:T(8,128)(2,1)} %rows_hbm.1, bf16[48,128,256]{2,1,0:T(8,128)(2,1)} %cols_hbm.1, ...), custom_call_target="tpu_custom_call" | custom-call | tf_op jit(solution)/shard_map/major/pallas_call | solution.py:382
  150.0 1.7 %copy.11 = f32[2,32,1024]{2,1,0:T(8,128)} copy(f32[2,32,1024]{2,1,0:T(8,128)} %get-tuple-element.4) | data formatting | bytes 524288
  151.7 1.5 %copy.12 = f32[48,2,256]{2,1,0:T(2,128)} copy(f32[48,2,256]{2,1,0:T(2,128)} %get-tuple-element.5) | data formatting | bytes 196608

commit v6 on v5

--- a/solution.py
+++ b/solution.py
@@ -270,7 +270,7 @@
                         total += sums[c, h, way, hops[way ^ h] - 1]
                 out_ref[c, :, h * chunk : (h + 1) * chunk] = total
 
-    batch = min(8, tiles)
+    batch = min(4, tiles)
     turns = tiles // batch
     lane = lax.broadcasted_iota(jnp.int32, (1, 128), 1)
     grid_row = lax.broadcasted_iota(jnp.int32, (tile_rows, 128), 0)
@@ -378,7 +378,7 @@
     hops = max(group // 2, 1)
     dma = pltpu.SemaphoreType.DMA
     back = (2, tiles, slots, sub_rows, sub_cols)
-    batch = min(8, tiles)
+    batch = min(4, tiles)
     return pl.pallas_call(
         functools.partial(major_kernel, tiles, group, slots),
         out_shape=[

time: 155 us -> 155 us (level)
  no operation moved by 1% of the time
where the time goes in v6:
time: 155 us; the launch traced here: 154 us
  Pallas kernels  150 us (97%)
  local copies, waits for them, and re-layouts  3.21 us (2%)
    pallas_call x1, Pallas kernels, shards(): pl.pallas_call(functools.partial(major_kernel, tiles, group, slots), out_...  150 us
    unnamed x2, local copies, waits for them, and re-layouts  3.21 us

profile of v6, /device:TPU:6, one launch (start us, length us, event | category | flops | bytes accessed | tf_op | source)
XLA Modules:
  0.0 154.3 jit_solution(6533431326334927520)
XLA Ops:
  0.6 150.5 %major.1 = (f32[2,32,1024]{2,1,0:T(8,128)}, f32[48,2,256]{2,1,0:T(2,128)}) custom-call(s32[1,48]{1,0:T(1,128)} %bitcast.3, s32[1,48]{1,0:T(1,128)} %bitcast.4, s32[1,48]{1,0:T(1,128)} %bitcast.5, bf16[2,32,1024]{2,1,0:T(8,128)(2,1)} %model_hbm.1, bf16[48,32,256]{2,1,0:T(8,128)(2,1)} %rows_hbm.1, bf16[48,128,256]{2,1,0:T(8,128)(2,1)} %cols_hbm.1, ...), custom_call_target="tpu_custom_call" | custom-call | tf_op jit(solution)/shard_map/major/pallas_call | solution.py:382
  151.1 1.7 %copy.11 = f32[2,32,1024]{2,1,0:T(8,128)} copy(f32[2,32,1024]{2,1,0:T(8,128)} %get-tuple-element.4) | data formatting | bytes 524288
  152.8 1.5 copy.12
